TPU v7x, 256 devices: a whole 4x4x8 slice. The times are simulated.
256 devices in a mesh: fft: 32 (over z, x_lo, core), grp: 8 (over y, x_hi).
Axes of the slice: x: 4 (x_hi: 2, x_lo: 2; x = x_hi * 2 + x_lo), y: 4, z: 8, core: 2. Of those that a mesh axis runs over, the one named last changes fastest.
Arguments:
- psi_valence: bfloat16 [16, 64, 4096], P(None, 'fft'), may hold values from -6 to 6
- psi_conduction: bfloat16 [384, 64, 4096], P(None, 'fft'), may hold values from -6 to 6
- energy_valence: float32 [16], replicated, may hold values from -6 to -0.5
- energy_conduction: float32 [384], replicated, may hold values from 0.5 to 8
- pair_valence: int32 [320], P('grp'), may hold values from 0 to 15
- pair_conduction: int32 [320], P('grp'), may hold values from 0 to 383
- g_index: int32 [6144], replicated, may hold values from 0 to 262143, as said below
Outputs:
- chi_real: float32 [6144, 6144], P('fft', 'grp')
- chi_imag: float32 [6144, 6144], P('fft', 'grp')
Inputs may be any that keep to these rules, and one draw needn't show every extreme that they name: `g_index`: the 6144 entries are distinct grid points in flat order a * 64 * 64 + b * 64 + c.
All inputs are finite; a program needn't handle non-finite values.
Results may differ from a plain program's by a relative error of at most 0.0041.
Values may be sent and summed in bfloat16 or wider, within the bound.
A program may use at most 128 MiB of HBM per device.

v0:
```python
import math

import jax
import jax.numpy as jnp
from jax import lax
from jax.sharding import PartitionSpec as P

HIGHEST = lax.Precision.HIGHEST


def phase_table(length):
    steps_idx = jnp.arange(length, dtype=jnp.int32)
    turn_count = (steps_idx[:, None] * steps_idx[None, :] % length).astype(jnp.float32)
    angles = turn_count * (2.0 * math.pi / length)
    return (jnp.cos(angles), jnp.sin(angles))


def rotate(real_part, imag_part, cos_table, sin_table, pattern):
    real_cos = jnp.einsum(
        pattern, real_part, cos_table, precision=HIGHEST, preferred_element_type=jnp.float32
    )
    real_sin = jnp.einsum(
        pattern, real_part, sin_table, precision=HIGHEST, preferred_element_type=jnp.float32
    )
    imag_cos = jnp.einsum(
        pattern, imag_part, cos_table, precision=HIGHEST, preferred_element_type=jnp.float32
    )
    imag_sin = jnp.einsum(
        pattern, imag_part, sin_table, precision=HIGHEST, preferred_element_type=jnp.float32
    )
    return (real_cos + imag_sin, imag_cos - real_sin)


def per_device(
    psi_valence,
    psi_conduction,
    energy_valence,
    energy_conduction,
    pair_valence,
    pair_conduction,
    g_index,
):
    planes = psi_valence.shape[1]
    plane_size = psi_valence.shape[2]
    length = math.isqrt(plane_size)
    pair_count = pair_valence.shape[0]
    cos_table, sin_table = phase_table(length)
    density = psi_valence[pair_valence].astype(jnp.float32) * psi_conduction[
        pair_conduction
    ].astype(jnp.float32)
    density = density.reshape(pair_count, planes, length, length)
    z_real = jnp.einsum(
        "pxyz,kz->pxyk", density, cos_table, precision=HIGHEST, preferred_element_type=jnp.float32
    )
    z_imag = -jnp.einsum(
        "pxyz,kz->pxyk", density, sin_table, precision=HIGHEST, preferred_element_type=jnp.float32
    )
    y_real, y_imag = rotate(z_real, z_imag, cos_table, sin_table, "pxyz,ky->pxkz")
    x_index = g_index // plane_size
    in_plane = g_index % plane_size
    pen_real, pen_imag = (
        lax.all_to_all(y_real, "fft", split_axis=2, concat_axis=1, tiled=True),
        lax.all_to_all(y_imag, "fft", split_axis=2, concat_axis=1, tiled=True),
    )
    k_real, k_imag = rotate(pen_real, pen_imag, cos_table, sin_table, "pxyz,kx->pkyz")
    width_y = pen_real.shape[2]
    y_start = lax.axis_index("fft") * width_y
    y_value = in_plane // length
    inside = (y_value >= y_start) & (y_value < y_start + width_y)
    local_index = x_index * (width_y * length) + (y_value - y_start) * length + in_plane % length
    local_index = jnp.where(inside, local_index, 0)
    keep_mask = inside.astype(jnp.float32)
    part_real = k_real.reshape(pair_count, -1)[:, local_index] * keep_mask
    part_imag = k_imag.reshape(pair_count, -1)[:, local_index] * keep_mask
    weight = 2.0 / (energy_conduction[pair_conduction] - energy_valence[pair_valence])
    factor = jnp.sqrt(weight) * (pair_count * lax.axis_size("grp")) ** (-0.25) * length ** (-1.5)
    sum_real, sum_imag = lax.psum((part_real, part_imag), "fft")
    scaled_real = (sum_real * factor[:, None]).astype(jnp.bfloat16)
    scaled_imag = (sum_imag * factor[:, None]).astype(jnp.bfloat16)
    sphere_total = g_index.shape[0]
    row_width = sphere_total // lax.axis_size("fft")
    row_start = lax.axis_index("fft") * row_width
    col_width = sphere_total // lax.axis_size("grp")
    col_real, col_imag = (
        lax.all_to_all(scaled_real, "grp", split_axis=1, concat_axis=0, tiled=True),
        lax.all_to_all(scaled_imag, "grp", split_axis=1, concat_axis=0, tiled=True),
    )
    own_real = lax.dynamic_slice_in_dim(scaled_real, row_start, row_width, 1)
    own_imag = lax.dynamic_slice_in_dim(scaled_imag, row_start, row_width, 1)
    zero_block = jnp.zeros((row_width, col_width), jnp.float32)
    pieces = (
        lax.all_gather(own_real, "grp", axis=0, tiled=True),
        lax.all_gather(own_imag, "grp", axis=0, tiled=True),
    )
    left_sum = jnp.concatenate([pieces[0], pieces[1]], 0)
    left_cross = jnp.concatenate([pieces[0], -pieces[1]], 0)
    right_sum = jnp.concatenate([col_real, col_imag], 0)
    right_cross = jnp.concatenate([col_imag, col_real], 0)
    real_add = jnp.einsum("pg,ph->gh", left_sum, right_sum, preferred_element_type=jnp.float32)
    imag_add = jnp.einsum("pg,ph->gh", left_cross, right_cross, preferred_element_type=jnp.float32)
    chi_real = (zero_block, zero_block)[0] - real_add
    return (chi_real, imag_add)


def solution(mesh):
    placed = (P(None, "fft", None), P(None, "fft", None), P(), P(), P("grp"), P("grp"), P())
    return jax.shard_map(
        per_device,
        mesh=mesh,
        in_specs=placed,
        out_specs=(P("fft", "grp"), P("fft", "grp")),
        check_vma=False,
    )
```

profile of v0, /device:TPU:98, one launch (start us, length us, event | category | flops | bytes accessed | tf_op | source)
XLA Modules:
  0.0 558.7 jit_solution(12473012764660378757)
XLA Ops:
  10.0 4.6 gather_fusion.1
  15.9 2.8 mul.160
  22.6 5.0 fusion.34
  32.7 3.5 copy.39
  36.3 5.2 reshape.89
  41.5 8.8 %all-to-all-start.1 = ((f32[32,1,10240]{2,1,0:T(1,128)}), f32[32,1,10240]{2,1,0:T(1,128)}, u32[]{:S(2)}, u32[]{:S(2)}) async-start(f32[32,1,10240]{2,1,0:T(1,128)} %reshape.89), calls=%async_computation.1 | async-start | bytes 2621440 | tf_op jit(solution)/shard_map/all_to_all | solution.py:63
  57.5 3.8 reshape.91
  61.3 20.3 %all-to-all-done.1 = f32[32,1,10240]{2,1,0:T(1,128)} async-done(((f32[32,1,10240]{2,1,0:T(1,128)}), f32[32,1,10240]{2,1,0:T(1,128)}, u32[]{:S(2)}, u32[]{:S(2)}) %all-to-all-start.1) | async-done | bytes 1310752 | tf_op jit(solution)/shard_map/all_to_all | solution.py:63
  81.6 7.4 %all-to-all-start = ((f32[32,1,10240]{2,1,0:T(1,128)}), f32[32,1,10240]{2,1,0:T(1,128)}, u32[]{:S(2)}, u32[]{:S(2)}) async-start(f32[32,1,10240]{2,1,0:T(1,128)} %reshape.91), calls=%async_computation | async-start | bytes 2621440 | tf_op jit(solution)/shard_map/all_to_all | solution.py:62
  89.9 5.1 reduce.1
  94.9 3.4 reshape.90
  98.3 3.2 copy.22
  101.6 18.7 %all-to-all-done = f32[32,1,10240]{2,1,0:T(1,128)} async-done(((f32[32,1,10240]{2,1,0:T(1,128)}), f32[32,1,10240]{2,1,0:T(1,128)}, u32[]{:S(2)}, u32[]{:S(2)}) %all-to-all-start) | async-done | bytes 1310752 | tf_op jit(solution)/shard_map/all_to_all | solution.py:62
  120.3 6.1 %reduce = f32[32,10240]{1,0:T(8,128)} reduce(f32[32,1,10240]{2,1,0:T(1,128)} %all-to-all-done, f32[]{:T(128)} %broadcast.127), dimensions={1}, to_apply=%all_to_all.54.reduce_sub_computation | reduce | bytes 2621444 | tf_op jit(solution)/shard_map/all_to_all | solution.py:62
  126.4 4.4 reshape.92
  130.8 3.2 copy.20
  134.0 2.6 fusion.30
  136.6 2.6 fusion.27
  139.2 4.3 add_bitcast_fusion
  143.5 4.3 subtract_bitcast_fusion
  147.8 5.0 copy.34
  152.8 3.5 copy.33
  156.3 18.5 %gather_fusion.5 = f32[6144,40]{1,0:T(8,128)S(1)} fusion(f32[40,8192]{0,1:T(8,128)} %bitcast.76, s32[6144]{0:T(1024)S(1)} %fusion.43), kind=kCustom, calls=%fused_computation.5 | custom fusion | bytes 1990656 | tf_op jit(solution)/shard_map/gather | solution.py:74
  174.8 23.3 %gather_fusion.2 = f32[6144,40]{1,0:T(8,128)} fusion(f32[40,8192]{0,1:T(8,128)} %bitcast.75, s32[6144]{0:T(1024)S(1)} %fusion.43), kind=kCustom, calls=%fused_computation.2 | custom fusion | bytes 1990656 | tf_op jit(solution)/shard_map/gather | solution.py:73
  198.0 4.6 multiply_bitcast_fusion.1
  204.9 241.8 %all-reduce.3.cloned.1.call-done = (f32[40,6144]{0,1:T(8,128)}, f32[40,6144]{0,1:T(8,128)}) async-done(((f32[40,6144]{0,1:T(8,128)}, f32[40,6144]{0,1:T(8,128)}), (f32[40,6144]{0,1:T(8,128)}, f32[40,6144]{0,1:T(8,128)})) %all-reduce.3.cloned.1.call-update) | async-done | bytes 1966096 | tf_op jit(solution)/shard_map/psum | solution.py:77
  446.7 3.3 multiply_convert_fusion.1
  451.3 5.6 %all-to-all-start.3 = ((bf16[40,8,768]{2,0,1:T(8,128)(2,1)}), bf16[40,8,768]{2,0,1:T(8,128)(2,1)}, u32[]{:S(2)}, u32[]{:S(2)}) async-start(bf16[40,8,768]{2,0,1:T(8,128)(2,1)} %copy.30), calls=%async_computation.3 | async-start | bytes 983040 | tf_op jit(solution)/shard_map/all_to_all | solution.py:86
  458.3 10.4 %all-to-all-done.3 = bf16[40,8,768]{2,0,1:T(8,128)(2,1)} async-done(((bf16[40,8,768]{2,0,1:T(8,128)(2,1)}), bf16[40,8,768]{2,0,1:T(8,128)(2,1)}, u32[]{:S(2)}, u32[]{:S(2)}) %all-to-all-start.3) | async-done | bytes 491552 | tf_op jit(solution)/shard_map/all_to_all | solution.py:86
  468.7 4.1 all-to-all-start.2
  473.0 39.0 %all_gather.7 = bf16[320,192]{1,0:T(8,128)(2,1)S(1)} all-gather(bf16[40,192]{1,0:T(8,128)(2,1)S(1)} %copy.28), channel_id=1, replica_groups=mesh['fft'=32,'grp'=8] {'grp'}, dimensions={0}, use_global_device_ids=true | all-gather | bytes 138240 | tf_op jit(solution)/shard_map/all_gather | solution.py:93
  512.1 34.6 %all_gather.6 = bf16[320,192]{1,0:T(8,128)(2,1)S(1)} all-gather(bf16[40,192]{1,0:T(8,128)(2,1)S(1)} %copy.25), channel_id=1, replica_groups=mesh['fft'=32,'grp'=8] {'grp'}, dimensions={0}, use_global_device_ids=true | all-gather | bytes 138240 | tf_op jit(solution)/shard_map/all_gather | solution.py:92
  (47 shorter events, 31.1 us)
Async XLA Ops:
  7.2 1.0 copy-start
  18.7 1.5 copy-start.4
  22.6 7.6 %copy-start.5 = (f32[40,2,64,64]{3,2,1,0:T(8,128)}, f32[40,2,64,64]{3,2,1,0:T(8,128)S(1)}, u32[]{:S(2)}) copy-start(f32[40,2,64,64]{3,2,1,0:T(8,128)S(1)} %fusion.25) | copy-start | bytes 3932164
  41.5 40.1 %all-to-all-start.1 = ((f32[32,1,10240]{2,1,0:T(1,128)}), f32[32,1,10240]{2,1,0:T(1,128)}, u32[]{:S(2)}, u32[]{:S(2)}) async-start(f32[32,1,10240]{2,1,0:T(1,128)} %reshape.89), calls=%async_computation.1 | async-start | bytes 2621440 | tf_op jit(solution)/shard_map/all_to_all | solution.py:63
  50.3 2.6 copy-start.6
  57.5 31.7 %copy-start.8 = (s32[6144]{0:T(1024)S(1)}, s32[6144]{0:T(1024)}, u32[]{:S(2)}) copy-start(s32[6144]{0:T(1024)} %param.13) | copy-start | bytes 73732
  81.6 38.6 %all-to-all-start = ((f32[32,1,10240]{2,1,0:T(1,128)}), f32[32,1,10240]{2,1,0:T(1,128)}, u32[]{:S(2)}, u32[]{:S(2)}) async-start(f32[32,1,10240]{2,1,0:T(1,128)} %reshape.91), calls=%async_computation | async-start | bytes 2621440 | tf_op jit(solution)/shard_map/all_to_all | solution.py:62
  89.0 357.7 %all-reduce.3.cloned.1.call-start = ((), (), s32[]{:S(2)}) async-start(), calls=%async_computation.4 | async-start | bytes 12582912 | tf_op jit(solution)/shard_map/psum | solution.py:77
  147.8 5.0 copy-start.7
  202.6 0.7 copy-start.3
  202.6 1.5 copy-start.2
  451.3 17.4 %all-to-all-start.3 = ((bf16[40,8,768]{2,0,1:T(8,128)(2,1)}), bf16[40,8,768]{2,0,1:T(8,128)(2,1)}, u32[]{:S(2)}, u32[]{:S(2)}) async-start(bf16[40,8,768]{2,0,1:T(8,128)(2,1)} %copy.30), calls=%async_computation.3 | async-start | bytes 983040 | tf_op jit(solution)/shard_map/all_to_all | solution.py:86
  468.7 78.0 %all-to-all-start.2 = ((bf16[40,8,768]{2,0,1:T(8,128)(2,1)}), bf16[40,8,768]{2,0,1:T(8,128)(2,1)}, u32[]{:S(2)}, u32[]{:S(2)}) async-start(bf16[40,8,768]{2,0,1:T(8,128)(2,1)} %copy.29), calls=%async_computation.2 | async-start | bytes 983040 | tf_op jit(solution)/shard_map/all_to_all | solution.py:85
  546.7 4.9 copy-start.1
Sparse Core Ops, SparseCore 0:
  202.7 243.8 all-reduce.2
where the time goes:
time: 563 us; the launch traced here: 559 us
  waiting for transfers between devices  291 us (52%)
  local copies, waits for them, and re-layouts  95.7 us (17%)
  blocking collectives  73.7 us (13%)
  matrix products  36.3 us (6%)
  starting transfers between devices  26.1 us (5%)
  other arithmetic  21.2 us (4%)
  between operations  14.6 us (3%)
    psum x1, waiting for transfers between devices, per_device(): sum_real, sum_imag = lax.psum((part_real, part_imag), 'fft')  242 us
    all_gather x1, blocking collectives, per_device(): lax.all_gather(own_imag, 'grp', axis=0, tiled=True)  39 us
    all_gather x1, blocking collectives, per_device(): lax.all_gather(own_real, 'grp', axis=0, tiled=True)  34.6 us
    gather x1, local copies, waits for them, and re-layouts, per_device(): part_real = k_real.reshape(pair_count, -1)[:, local_index] * keep_mask  23.3 us
    all_to_all x1, waiting for transfers between devices, per_device(): lax.all_to_all(y_imag, 'fft', split_axis=2, concat_axis=1, tiled=True)  20.3 us
    unnamed x22, local copies, waits for them, and re-layouts  19.3 us
    all_to_all x1, waiting for transfers between devices, per_device(): lax.all_to_all(y_real, 'fft', split_axis=2, concat_axis=1, tiled=True)  18.7 us
    gather x1, local copies, waits for them, and re-layouts, per_device(): part_imag = k_imag.reshape(pair_count, -1)[:, local_index] * keep_mask  18.5 us
  transfers between devices with their start and end apart: 5, of which 4 were waited for; matrix products, arithmetic and copies ran while one was open for 5% of the time, Pallas kernels for 0%

commit v1 on v0

v1 whole, which is shorter than its diff:
```python
import functools
import math

import jax
import jax.numpy as jnp
import ml_dtypes
import numpy as np
from jax import lax
from jax.experimental import pallas as pl
from jax.experimental.pallas import tpu as pltpu
from jax.sharding import PartitionSpec as P

NG = 64
HALF_C = 34
KEYS = HALF_C * NG
PAIRS = 40
BOTH = 2 * PAIRS
CHIPS = 16
CHIP_POINTS = 384
BF16 = jnp.bfloat16
F32 = jnp.float32
MESH = pl.DeviceIdType.MESH


def split_table(table):
    high = table.astype(ml_dtypes.bfloat16)
    low = (table - high.astype(np.float64)).astype(ml_dtypes.bfloat16)
    return high, low


def table_z():
    c, z = np.arange(33)[:, None], np.arange(NG)[None, :]
    angle = 2 * np.pi * ((c * z) % NG) / NG
    table = np.zeros((HALF_C, 4, 2, 4, NG))
    for y in range(4):
        table[:33, y, 0, y] = np.cos(angle)
        table[:33, y, 1, y] = -np.sin(angle)
    high, low = split_table(table.reshape(HALF_C * 8, 4 * NG))
    return np.concatenate([high, high, low], 1)


def table_y():
    y, b = np.arange(NG)[:, None], np.arange(NG)[None, :]
    angle = 2 * np.pi * ((y * b) % NG) / NG
    table = np.zeros((NG, 2, 2, NG))
    table[:, 0, 0], table[:, 0, 1] = np.cos(angle), -np.sin(angle)
    table[:, 1, 0], table[:, 1, 1] = np.sin(angle), np.cos(angle)
    high, low = split_table(table.reshape(2 * NG, 2 * NG))
    return np.concatenate([high, high, low], 0)


def table_x():
    angle = 2 * np.pi * np.arange(NG) / NG
    table = np.zeros((8, NG), np.float32)
    table[0], table[1] = np.cos(angle), np.sin(angle)
    return table


def split(x):
    high = x.astype(BF16)
    return high, (x - high.astype(F32)).astype(BF16)


def dot(a, b, contract, precision=None):
    return lax.dot_general(
        a, b, (contract, ((), ())), precision=precision, preferred_element_type=F32
    )


def front_kernel(
    total_pairs,
    pair_c, pair_v, energy_c, energy_v, plane,
    psi_c, psi_v, wz, wy, wx, g_index,
    out,
    band_v, band_c, density, z_part, y_part, sem,
):
    copy_v = pltpu.make_async_copy(psi_v, band_v, sem.at[1])
    copy_v.start()

    def fetch(p, _):
        pltpu.make_async_copy(psi_c.at[pair_c[p]], band_c.at[p], sem.at[0]).start()
        return 0

    lax.fori_loop(0, PAIRS, fetch, 0)

    row = lax.broadcasted_iota(jnp.int32, (BOTH, 128), 0)
    row = jnp.where(row >= PAIRS, row - PAIRS, row)

    def gaps(p, gap):
        return jnp.where(row == p, energy_c[pair_c[p]] - energy_v[pair_v[p]], gap)

    gap = lax.fori_loop(0, PAIRS, gaps, jnp.ones((BOTH, 128), F32))
    factor = jnp.sqrt(2.0 / gap) * (total_pairs ** (-0.25) * NG ** (-1.5))

    copy_v.wait()
    pltpu.make_async_copy(psi_c.at[pl.ds(0, PAIRS)], band_c, sem.at[0]).wait()

    def multiply(p, _):
        start = pl.multiple_of(p * NG, NG)
        density[pl.ds(start, NG), :] = band_v[pair_v[p]].astype(F32) * band_c[p].astype(F32)
        return 0

    lax.fori_loop(0, PAIRS, multiply, 0)

    def along_z(i, _):
        lines = []
        for t in range(2):
            lines.append(jnp.concatenate(
                [density[pl.ds(4 * i + 2 * t + x, PAIRS, stride=NG), :] for x in range(2)], 0
            ))
        high, low = split(jnp.concatenate(lines, 1))
        lines = jnp.concatenate([high, low, high], 1)
        result = dot(wz[...], lines, ((1,), (1,)))
        start = pl.multiple_of(8 * i, 8)
        z_part[:, pl.ds(start, 8), 0:BOTH] = result.reshape(HALF_C, 8, BOTH)
        return 0

    lax.fori_loop(0, NG // 4, along_z, 0)

    lane = lax.broadcasted_iota(jnp.int32, (BOTH, 128), 1)

    def along_y(k, most):
        lines = jnp.concatenate([z_part[2 * k + c].T[0:BOTH] for c in range(2)], 0)
        high, low = split(lines)
        result = dot(jnp.concatenate([high, low, high], 1), wy[...], ((1,), (0,)))
        first, second = result[0:BOTH], result[BOTH:]
        real = jnp.where(lane < NG, first, pltpu.roll(second, NG, 1)) * factor
        imag = jnp.where(lane < NG, pltpu.roll(first, NG, 1), second) * factor
        start = pl.multiple_of(128 * k, 128)
        for i, part in enumerate(split(real) + split(imag)):
            place = (0, 2, 1, 3)[i] * BOTH
            y_part[place:place + BOTH, pl.ds(start, 128)] = part
        size = jnp.abs(real) + jnp.abs(imag)
        return jnp.maximum(most, size[0:PAIRS] + size[PAIRS:])

    most = lax.fori_loop(0, HALF_C // 2, along_y, jnp.zeros((PAIRS, 128), F32))
    most = jnp.max(jnp.max(most, 0, keepdims=True), 1, keepdims=True)
    level = jnp.floor(jnp.log2(jnp.maximum(most, 1e-30) * 1.001)) + 1.0
    level_rows = jnp.broadcast_to(level, (8, 128))
    up = jnp.exp2(15.0 - level)

    x0 = plane[0]
    half_lane = lax.broadcasted_iota(jnp.int32, (PAIRS, 128), 1) < NG
    key_row = lax.broadcasted_iota(jnp.int16, (KEYS, CHIP_POINTS), 0)
    turn_row = lax.broadcasted_iota(jnp.int32, (NG, 2 * CHIP_POINTS), 0)

    def select(j, _):
        g = g_index[0:1, pl.ds(pl.multiple_of(j * CHIP_POINTS, 128), CHIP_POINTS)]
        a, b, c = g >> 12, (g >> 6) & 63, g & 63
        mirror = c > 32
        a = jnp.where(mirror, (NG - a) & 63, a)
        b = jnp.where(mirror, (NG - b) & 63, b)
        c = jnp.where(mirror, NG - c, c)
        key = (c * NG + b).astype(jnp.int16)
        chosen = jnp.where(key_row == key, BF16(1), BF16(0))
        picked = dot(y_part[...], chosen, ((1,), (0,)))
        picked = picked[0:2 * BOTH] + picked[2 * BOTH:]
        re0, re1, im0, im1 = (picked[i * PAIRS:(i + 1) * PAIRS] for i in range(4))
        turns = jnp.concatenate([(a * x0) & 63, (a * (x0 + 1)) & 63], 1)
        phase = dot(wx[...], (turn_row == turns).astype(F32), ((1,), (0,)), lax.Precision.HIGHEST)
        cos0, cos1 = phase[0:1, 0:CHIP_POINTS], phase[0:1, CHIP_POINTS:]
        sin0, sin1 = phase[1:2, 0:CHIP_POINTS], phase[1:2, CHIP_POINTS:]
        sign = jnp.where(mirror, -up, up)
        real = (cos0 * re0 + sin0 * im0 + cos1 * re1 + sin1 * im1) * up
        imag = (cos0 * im0 - sin0 * re0 + cos1 * im1 - sin1 * re1) * sign
        real, imag = jnp.floor(real + 0.5), jnp.floor(imag + 0.5)
        middle_re, middle_im = real[:, 128:256], imag[:, 128:256]
        for core in range(2):
            if core == 0:
                middle = jnp.where(half_lane, middle_re, pltpu.roll(middle_im, NG, 1))
            else:
                middle = jnp.where(half_lane, pltpu.roll(middle_re, NG, 1), middle_im)
            lanes = slice(256 * core, 256 * core + 128)
            slab = jnp.concatenate([real[:, lanes], imag[:, lanes], middle, level_rows], 0)
            out[core, j] = slab.astype(jnp.int32).astype(jnp.int16)
        return 0

    lax.fori_loop(0, CHIPS, select, 0)


def front(pair_c, pair_v, energy_c, energy_v, plane, psi_c, psi_v, g_index, total_pairs):
    smem = pl.BlockSpec(memory_space=pltpu.SMEM)
    vmem = pl.BlockSpec(memory_space=pltpu.VMEM)
    anywhere = pl.BlockSpec(memory_space=pl.ANY)
    return pl.pallas_call(
        functools.partial(front_kernel, total_pairs),
        out_shape=jax.ShapeDtypeStruct((2, CHIPS, 128, 128), jnp.int16),
        in_specs=[smem] * 5 + [anywhere] * 2 + [vmem] * 4,
        out_specs=vmem,
        scratch_shapes=[
            pltpu.VMEM(psi_v.shape, BF16),
            pltpu.VMEM((PAIRS, NG, 128), BF16),
            pltpu.VMEM((PAIRS * NG, 128), F32),
            pltpu.VMEM((HALF_C, 128, 128), F32),
            pltpu.VMEM((4 * BOTH, KEYS), BF16),
            pltpu.SemaphoreType.DMA((2,)),
        ],
        compiler_params=pltpu.CompilerParams(vmem_limit_bytes=40 * 1024 * 1024),
    )(
        pair_c, pair_v, energy_c, energy_v, plane, psi_c, psi_v,
        jnp.asarray(table_z()), jnp.asarray(table_y()), jnp.asarray(table_x()), g_index,
    )


def exchange_kernel(
    q, chi_real, chi_imag,
    core_in, chip_out, chip_in, block, z_blocks, row_blocks, col_blocks,
    core_send, core_recv, chip_send, chip_recv, z_send, z_recv,
    row_send, row_recv, plane_send, plane_recv, relay_send, relay_recv,
):
    f, g = lax.axis_index("fft"), lax.axis_index("grp")
    core, chip, z = f % 2, f // 2, f // 4
    x = chip % 2
    sibling = f + 1 - 2 * core

    def remote(src, dst, send, recv, to):
        return pltpu.make_async_remote_copy(
            src_ref=src, dst_ref=dst, send_sem=send, recv_sem=recv,
            device_id=to, device_id_type=MESH,
        )

    barrier = pltpu.get_barrier_semaphore()
    pl.semaphore_signal(barrier, 1, device_id=(sibling, g), device_id_type=MESH)

    def greet_chip(k, _):
        to = ((2 * chip + 2 * k) % 32 + core, g)
        pl.semaphore_signal(barrier, 1, device_id=to, device_id_type=MESH)
        return 0

    lax.fori_loop(1, CHIPS, greet_chip, 0)

    def greet_plane(k, _):
        to = (z * 4 + (k % 2) * 2 + core, (g + k // 2) % 8)
        pl.semaphore_signal(barrier, 1, device_id=to, device_id_type=MESH)
        return 0

    lax.fori_loop(2, 16, greet_plane, 0)
    pl.semaphore_wait(barrier, 30)

    def to_sibling(j):
        return remote(q.at[1 - core, j], core_in.at[j], core_send.at[j], core_recv.at[j], (sibling, g))

    def send_core(k, _):
        to_sibling((chip + k) % CHIPS).start()
        return 0

    lax.fori_loop(1, CHIPS + 1, send_core, 0)

    tail = lax.broadcasted_iota(jnp.int32, (128, 128), 0) >= 120

    def to_chip(j):
        return remote(
            chip_out.at[j], chip_in.at[chip], chip_send.at[j], chip_recv.at[chip], (2 * j + core, g)
        )

    def add_core(k, _):
        j = (chip + k) % CHIPS
        to_sibling(j).wait_recv()
        own, other = q[core, j].astype(jnp.int32).astype(F32), core_in[j].astype(jnp.int32).astype(F32)
        own_level, other_level = own[120:121], other[120:121]
        level = jnp.maximum(own_level, other_level) + 1.0
        total = own * jnp.exp2(own_level - level) + other * jnp.exp2(other_level - level)
        total = jnp.where(tail, level, jnp.floor(total + 0.5))
        chip_out[j] = total.astype(jnp.int32).astype(jnp.int16)

        @pl.when(k < CHIPS)
        def _():
            to_chip(j).start()

        return 0

    lax.fori_loop(1, CHIPS + 1, add_core, 0)

    def scaled(slab):
        slab = slab.astype(jnp.int32).astype(F32)
        return slab * jnp.exp2(slab[120:121] - 15.0)

    def add_chip(k, total):
        j = (chip + k) % CHIPS
        remote(
            chip_out.at[j], chip_in.at[j], chip_send.at[j], chip_recv.at[j], (2 * j + core, g)
        ).wait_recv()
        return total + scaled(chip_in[j])

    total = lax.fori_loop(1, CHIPS, add_chip, scaled(chip_out[chip]))
    block[...] = jnp.where(tail, 0.0, total).astype(BF16)

    def to_z(k):
        other = (z + k) % 8
        return remote(
            block, z_blocks.at[z], z_send.at[other], z_recv.at[z], (other * 4 + x * 2 + core, g)
        )

    def to_row(k):
        other = (g + k) % 8
        return remote(block, row_blocks.at[g], row_send.at[other], row_recv.at[g], (f, other))

    def send_block(k, _):
        to_z(k).start()
        to_row(k).start()
        return 0

    lax.fori_loop(1, 8, send_block, 0)
    z_blocks[z] = block[...]
    row_blocks[g] = block[...]

    def to_plane(layer, to_x):
        return remote(
            z_blocks.at[layer], col_blocks.at[core, x, g],
            plane_send.at[layer, to_x], plane_recv.at[x, g], (z * 4 + to_x * 2 + core, layer),
        )

    def stays(layer, to_x):
        return jnp.logical_and(layer == g, to_x == x)

    def spread(k, _):
        layer = (z + (k + 1) // 2 * (1 - 2 * (k % 2)) + 8) % 8

        @pl.when(k > 0)
        def _():
            remote(
                block, z_blocks.at[layer], z_send.at[layer], z_recv.at[layer],
                (layer * 4 + x * 2 + core, g),
            ).wait_recv()

        for to_x in range(2):
            @pl.when(stays(layer, to_x))
            def _():
                col_blocks[core, x, g] = z_blocks[layer]

            @pl.when(jnp.logical_not(stays(layer, to_x)))
            def _():
                to_plane(layer, to_x).start()

        return 0

    lax.fori_loop(0, 8, spread, 0)

    def relay(side, from_x, from_g):
        return remote(
            col_blocks.at[side, from_x, from_g], col_blocks.at[side, from_x, from_g],
            relay_send.at[from_x, from_g], relay_recv.at[from_x, from_g], (sibling, g),
        )

    def pass_on(k, _):
        from_x, from_g = (x + k) % 2, (g + k // 2) % 8

        @pl.when(k > 0)
        def _():
            remote(
                z_blocks.at[0], col_blocks.at[core, from_x, from_g],
                plane_send.at[0, 0], plane_recv.at[from_x, from_g],
                (z * 4 + from_x * 2 + core, from_g),
            ).wait_recv()

        relay(core, from_x, from_g).start()
        return 0

    lax.fori_loop(0, 16, pass_on, 0)

    def row_arrives(k, _):
        other = (g + k) % 8
        remote(
            block, row_blocks.at[other], row_send.at[other], row_recv.at[other], (f, other)
        ).wait_recv()
        return 0

    lax.fori_loop(1, 8, row_arrives, 0)

    def relay_arrives(k, _):
        relay(1 - core, k % 2, k // 2).wait_recv()
        return 0

    lax.fori_loop(0, 16, relay_arrives, 0)

    half_lane = lax.broadcasted_iota(jnp.int32, (8 * PAIRS, 128), 1) < NG

    def gather(read):
        blocks = [read(i).astype(F32) for i in range(8)]
        return tuple(
            jnp.concatenate([b[s * PAIRS:(s + 1) * PAIRS] for b in blocks], 0) for s in range(3)
        )

    real, imag, middle = gather(lambda i: row_blocks[i])
    full = jnp.concatenate([real, imag], 0).astype(BF16)
    half = jnp.concatenate([middle, pltpu.roll(middle, NG, 1)], 0)[:, 0:NG].astype(BF16)
    full_row = pl.multiple_of(core * NG, NG)
    half_row = pl.multiple_of((1 - core) * 128, NG)
    for side in range(2):
        real0, imag0, middle0 = gather(lambda i: col_blocks[0, side, i])
        real2, imag2, middle2 = gather(lambda i: col_blocks[1, side, i])
        real1 = jnp.where(half_lane, middle0, pltpu.roll(middle2, NG, 1))
        imag1 = jnp.where(half_lane, pltpu.roll(middle0, NG, 1), middle2)
        real = jnp.concatenate([real0, real1, real2], 1)
        imag = jnp.concatenate([imag0, imag1, imag2], 1)
        right_sum = jnp.concatenate([real, imag], 0).astype(BF16)
        right_cross = jnp.concatenate([imag, -real], 0).astype(BF16)
        lanes = slice(side * CHIP_POINTS, (side + 1) * CHIP_POINTS)
        for left, rows in ((full, pl.ds(full_row, 128)), (half, pl.ds(half_row, NG))):
            chi_real[rows, lanes] = -dot(left, right_sum, ((0,), (0,)))
            chi_imag[rows, lanes] = dot(left, right_cross, ((0,), (0,)))

    def drain_chips(k, _):
        to_sibling((chip + k) % CHIPS).wait_send()

        @pl.when(k < CHIPS)
        def _():
            to_chip((chip + k) % CHIPS).wait_send()

        return 0

    lax.fori_loop(1, CHIPS + 1, drain_chips, 0)

    def drain_blocks(k, _):
        to_z(k).wait_send()
        to_row(k).wait_send()
        return 0

    lax.fori_loop(1, 8, drain_blocks, 0)

    def drain_plane(k, _):
        @pl.when(jnp.logical_not(stays(k // 2, k % 2)))
        def _():
            to_plane(k // 2, k % 2).wait_send()

        relay(core, k % 2, k // 2).wait_send()
        return 0

    lax.fori_loop(0, 16, drain_plane, 0)


def exchange(q, rows, columns):
    vmem = pl.BlockSpec(memory_space=pltpu.VMEM)
    dma = pltpu.SemaphoreType.DMA
    slabs = pltpu.VMEM((CHIPS, 128, 128), jnp.int16)
    blocks = pltpu.VMEM((8, 128, 128), BF16)
    shape = jax.ShapeDtypeStruct((rows, columns), F32)
    return pl.pallas_call(
        exchange_kernel,
        out_shape=(shape, shape),
        in_specs=[vmem],
        out_specs=(vmem, vmem),
        scratch_shapes=[
            slabs, slabs, slabs,
            pltpu.VMEM((128, 128), BF16),
            blocks, blocks,
            pltpu.VMEM((2, 2, 8, 128, 128), BF16),
            dma((CHIPS,)), dma((CHIPS,)), dma((CHIPS,)), dma((CHIPS,)),
            dma((8,)), dma((8,)), dma((8,)), dma((8,)),
            dma((8, 2)), dma((2, 8)), dma((2, 8)), dma((2, 8)),
        ],
        compiler_params=pltpu.CompilerParams(
            collective_id=0, has_side_effects=True, vmem_limit_bytes=40 * 1024 * 1024
        ),
    )(q)


def per_device(
    psi_valence,
    psi_conduction,
    energy_valence,
    energy_conduction,
    pair_valence,
    pair_conduction,
    g_index,
):
    def tiles(psi):
        bands = psi.shape[0]
        return psi.reshape(bands, 2, 32, 128).transpose(0, 2, 1, 3).reshape(bands, NG, 128)

    plane = (2 * lax.axis_index("fft")).astype(jnp.int32).reshape(1)
    slabs = front(
        pair_conduction, pair_valence, energy_conduction, energy_valence, plane,
        tiles(psi_conduction), tiles(psi_valence), g_index.reshape(1, -1),
        PAIRS * lax.axis_size("grp"),
    )
    points = g_index.shape[0]
    return exchange(slabs, points // lax.axis_size("fft"), points // lax.axis_size("grp"))


def solution(mesh):
    placed = (P(None, "fft", None), P(None, "fft", None), P(), P(), P("grp"), P("grp"), P())
    return jax.shard_map(
        per_device,
        mesh=mesh,
        in_specs=placed,
        out_specs=(P("fft", "grp"), P("fft", "grp")),
        check_vma=False,
    )
```

time: 563 us -> 88.2 us (0.16)
  the two profiles are of different devices: /device:TPU:98 before, /device:TPU:13 now
where the time goes in v1:
time: 88.2 us; the launch traced here: 86.7 us
  Pallas kernels  74.7 us (85%)
  local copies, waits for them, and re-layouts  11.3 us (13%)
    pallas_call x1, Pallas kernels, exchange(): pl.pallas_call(exchange_kernel, out_shape=(shape, shape), in_specs=[vmem]...  44.1 us
    pallas_call x1, Pallas kernels, front(): pl.pallas_call(functools.partial(front_kernel, total_pairs), out_shape=ja...  30.5 us
    unnamed x22, local copies, waits for them, and re-layouts  11.3 us

profile of v1, /device:TPU:13, one launch (start us, length us, event | category | flops | bytes accessed | tf_op | source)
XLA Modules:
  0.0 86.7 jit_solution(7822249542709831008)
XLA Ops:
  0.6 0.0 copy-start
  0.6 2.8 %copy-done = bf16[384,2,4096]{2,1,0:T(2,128)(2,1)S(1)} copy-done((bf16[384,2,4096]{2,1,0:T(2,128)(2,1)S(1)}, bf16[384,2,4096]{2,1,0:T(2,128)(2,1)}, u32[]{:S(2)}) %copy-start) | copy-done | bytes 6291480
  3.4 0.0 copy-start.1
  3.4 1.0 %copy-done.1 = bf16[272,768]{1,0:T(8,128)(2,1)S(1)} copy-done((bf16[272,768]{1,0:T(8,128)(2,1)S(1)}, bf16[272,768]{1,0:T(8,128)(2,1)}, u32[]{:S(2)}) %copy-start.1) | copy-done | bytes 417816
  4.4 0.0 copy-start.2
  4.4 0.9 %copy-done.2 = bf16[16,2,4096]{2,1,0:T(2,128)(2,1)S(1)} copy-done((bf16[16,2,4096]{2,1,0:T(2,128)(2,1)S(1)}, bf16[16,2,4096]{2,1,0:T(2,128)(2,1)}, u32[]{:S(2)}) %copy-start.2) | copy-done | bytes 262168
  5.4 0.0 copy-start.3
  5.4 0.9 %copy-done.3 = bf16[384,128]{1,0:T(8,128)(2,1)S(1)} copy-done((bf16[384,128]{1,0:T(8,128)(2,1)S(1)}, bf16[384,128]{1,0:T(8,128)(2,1)}, u32[]{:S(2)}) %copy-start.3) | copy-done | bytes 98328
  6.3 0.0 copy-start.4
  6.3 0.7 copy-done.4
  7.0 0.0 copy-start.5
  7.0 0.7 copy-done.5
  7.7 0.0 copy-start.6
  7.7 0.7 copy-done.6
  8.4 0.0 copy-start.7
  8.4 0.7 copy-done.7
  9.0 0.0 copy-start.8
  9.0 0.7 copy-done.8
  9.7 0.0 copy-start.9
  9.7 0.7 copy-done.9
  10.3 30.5 %shard_map.113.q = s16[2,16,128,128]{3,2,1,0:T(8,128)(2,1)S(1)} custom-call(s32[40]{0:T(128)S(1)} %copy-done.7, s32[40]{0:T(128)S(1)} %copy-done.8, f32[384]{0:T(512)S(1)} %copy-done.6, f32[16]{0:T(128)S(1)} %copy-done.9, s32[1]{0:T(128)} %bitcast.plane, bf16[384,64,128]{2,1,0:T(8,128)(2,1)S(1)} %bitcast.12, bf16[16,64,128]{2,1,0:T(8,128)(2,1)S(1)} %bitcast.13, ...), custom_call_target="tpu_custom_call" | custom-call | tf_op jit(solution)/shard_map/pallas_call | solution.py:185
  40.9 44.1 %shard_map.114 = (f32[192,768]{1,0:T(8,128)S(1)}, f32[192,768]{1,0:T(8,128)S(1)}) custom-call(s16[2,16,128,128]{3,2,1,0:T(8,128)(2,1)S(1)} %shard_map.113.q), custom_call_target="tpu_custom_call" | custom-call | tf_op jit(solution)/shard_map/pallas_call | solution.py:438
  85.0 0.8 copy.16
  85.9 0.8 copy.17
Async XLA Ops:
  0.6 2.8 %copy-start = (bf16[384,2,4096]{2,1,0:T(2,128)(2,1)S(1)}, bf16[384,2,4096]{2,1,0:T(2,128)(2,1)}, u32[]{:S(2)}) copy-start(bf16[384,2,4096]{2,1,0:T(2,128)(2,1)} %param.11) | copy-start | bytes 18874372
  3.4 1.0 %copy-start.1 = (bf16[272,768]{1,0:T(8,128)(2,1)S(1)}, bf16[272,768]{1,0:T(8,128)(2,1)}, u32[]{:S(2)}) copy-start(bf16[272,768]{1,0:T(8,128)(2,1)} %constant.14.clone.wz) | copy-start | bytes 1253380
  4.4 0.9 %copy-start.2 = (bf16[16,2,4096]{2,1,0:T(2,128)(2,1)S(1)}, bf16[16,2,4096]{2,1,0:T(2,128)(2,1)}, u32[]{:S(2)}) copy-start(bf16[16,2,4096]{2,1,0:T(2,128)(2,1)} %param.10) | copy-start | bytes 786436
  5.4 0.9 %copy-start.3 = (bf16[384,128]{1,0:T(8,128)(2,1)S(1)}, bf16[384,128]{1,0:T(8,128)(2,1)}, u32[]{:S(2)}) copy-start(bf16[384,128]{1,0:T(8,128)(2,1)} %constant.15.clone.wy) | copy-start | bytes 294916
  6.3 0.7 copy-start.4
  7.0 0.7 copy-start.5
  7.7 0.7 copy-start.6
  8.4 0.7 copy-start.7
  9.0 0.7 copy-start.8
  9.7 0.7 copy-start.9

commit v2 on v1

--- a/solution.py
+++ b/solution.py
@@ -17,6 +17,7 @@
 BOTH = 2 * PAIRS
 CHIPS = 16
 CHIP_POINTS = 384
+WIDE = 2 * CHIP_POINTS
 BF16 = jnp.bfloat16
 F32 = jnp.float32
 MESH = pl.DeviceIdType.MESH
@@ -67,21 +68,48 @@
     )
 
 
-def front_kernel(
+def kernel(
     total_pairs,
-    pair_c, pair_v, energy_c, energy_v, plane,
+    pair_c, pair_v, energy_c, energy_v,
     psi_c, psi_v, wz, wy, wx, g_index,
-    out,
-    band_v, band_c, density, z_part, y_part, sem,
+    chi_real, chi_imag,
+    band_v, band_c, density, z_part, y_part,
+    q, core_in, chip_out, chip_in, block, z_blocks, row_blocks, col_blocks, load,
+    core_send, core_recv, chip_send, chip_recv, z_send, z_recv,
+    row_send, row_recv, plane_send, plane_recv, relay_send, relay_recv,
 ):
-    copy_v = pltpu.make_async_copy(psi_v, band_v, sem.at[1])
+    f, g = lax.axis_index("fft"), lax.axis_index("grp")
+    core, chip, z = f % 2, f // 2, f // 4
+    x = chip % 2
+    sibling = f + 1 - 2 * core
+
+    copy_c = pltpu.make_async_copy(psi_c, band_c, load.at[0])
+    copy_v = pltpu.make_async_copy(psi_v, band_v, load.at[1])
+    copy_c.start()
     copy_v.start()
 
-    def fetch(p, _):
-        pltpu.make_async_copy(psi_c.at[pair_c[p]], band_c.at[p], sem.at[0]).start()
-        return 0
-
-    lax.fori_loop(0, PAIRS, fetch, 0)
+    def remote(src, dst, send, recv, to):
+        return pltpu.make_async_remote_copy(
+            src_ref=src, dst_ref=dst, send_sem=send, recv_sem=recv,
+            device_id=to, device_id_type=MESH,
+        )
+
+    barrier = pltpu.get_barrier_semaphore()
+    pl.semaphore_signal(barrier, 1, device_id=(sibling, g), device_id_type=MESH)
+
+    def greet_chip(k, _):
+        to = ((2 * chip + 2 * k) % 32 + core, g)
+        pl.semaphore_signal(barrier, 1, device_id=to, device_id_type=MESH)
+        return 0
+
+    lax.fori_loop(1, CHIPS, greet_chip, 0)
+
+    def greet_plane(k, _):
+        to = (z * 4 + (k % 2) * 2 + core, (g + k // 2) % 8)
+        pl.semaphore_signal(barrier, 1, device_id=to, device_id_type=MESH)
+        return 0
+
+    lax.fori_loop(2, 16, greet_plane, 0)
 
     row = lax.broadcasted_iota(jnp.int32, (BOTH, 128), 0)
     row = jnp.where(row >= PAIRS, row - PAIRS, row)
@@ -93,11 +121,13 @@
     factor = jnp.sqrt(2.0 / gap) * (total_pairs ** (-0.25) * NG ** (-1.5))
 
     copy_v.wait()
-    pltpu.make_async_copy(psi_c.at[pl.ds(0, PAIRS)], band_c, sem.at[0]).wait()
+    copy_c.wait()
 
     def multiply(p, _):
         start = pl.multiple_of(p * NG, NG)
-        density[pl.ds(start, NG), :] = band_v[pair_v[p]].astype(F32) * band_c[p].astype(F32)
+        density[pl.ds(start, NG), :] = (
+            band_v[pair_v[p]].astype(F32) * band_c[pair_c[p]].astype(F32)
+        )
         return 0
 
     lax.fori_loop(0, PAIRS, multiply, 0)
@@ -115,7 +145,7 @@
         z_part[:, pl.ds(start, 8), 0:BOTH] = result.reshape(HALF_C, 8, BOTH)
         return 0
 
-    lax.fori_loop(0, NG // 4, along_z, 0)
+    lax.fori_loop(0, NG // 4, along_z, 0, unroll=8)
 
     lane = lax.broadcasted_iota(jnp.int32, (BOTH, 128), 1)
 
@@ -133,20 +163,52 @@
         size = jnp.abs(real) + jnp.abs(imag)
         return jnp.maximum(most, size[0:PAIRS] + size[PAIRS:])
 
-    most = lax.fori_loop(0, HALF_C // 2, along_y, jnp.zeros((PAIRS, 128), F32))
+    most = lax.fori_loop(
+        0, HALF_C // 2, along_y, jnp.zeros((PAIRS, 128), F32), unroll=HALF_C // 2
+    )
     most = jnp.max(jnp.max(most, 0, keepdims=True), 1, keepdims=True)
     level = jnp.floor(jnp.log2(jnp.maximum(most, 1e-30) * 1.001)) + 1.0
     level_rows = jnp.broadcast_to(level, (8, 128))
     up = jnp.exp2(15.0 - level)
 
-    x0 = plane[0]
     half_lane = lax.broadcasted_iota(jnp.int32, (PAIRS, 128), 1) < NG
-    key_row = lax.broadcasted_iota(jnp.int16, (KEYS, CHIP_POINTS), 0)
-    turn_row = lax.broadcasted_iota(jnp.int32, (NG, 2 * CHIP_POINTS), 0)
-
-    def select(j, _):
-        g = g_index[0:1, pl.ds(pl.multiple_of(j * CHIP_POINTS, 128), CHIP_POINTS)]
-        a, b, c = g >> 12, (g >> 6) & 63, g & 63
+    key_row = lax.broadcasted_iota(jnp.int16, (KEYS, WIDE), 0)
+    turn_row = lax.broadcasted_iota(jnp.int32, (NG, 2 * WIDE), 0)
+    tail = lax.broadcasted_iota(jnp.int32, (128, 128), 0) >= 120
+
+    pl.semaphore_wait(barrier, 30)
+
+    def to_sibling(j):
+        return remote(q.at[1 - core, j], core_in.at[j], core_send.at[j], core_recv.at[j], (sibling, g))
+
+    def to_chip(j):
+        return remote(
+            chip_out.at[j], chip_in.at[chip], chip_send.at[j], chip_recv.at[chip], (2 * j + core, g)
+        )
+
+    def layer_of(k):
+        return (z + (4 - (k + 1) // 2) * (2 * (k % 2) - 1) + 8) % 8
+
+    def add_core(k):
+        for n in range(2):
+            j = 2 * layer_of(k) + n
+            to_sibling(j).wait_recv()
+            own = q[core, j].astype(jnp.int32).astype(F32)
+            other = core_in[j].astype(jnp.int32).astype(F32)
+            own_level, other_level = own[120:121], other[120:121]
+            level = jnp.maximum(own_level, other_level) + 1.0
+            total = own * jnp.exp2(own_level - level) + other * jnp.exp2(other_level - level)
+            total = jnp.where(tail, level, jnp.floor(total + 0.5))
+            chip_out[j] = total.astype(jnp.int32).astype(jnp.int16)
+
+            @pl.when(j != chip)
+            def _():
+                to_chip(j).start()
+
+    def select(k, _):
+        m = layer_of(k)
+        points = g_index[0:1, pl.ds(pl.multiple_of(m * WIDE, 128), WIDE)]
+        a, b, c = points >> 12, (points >> 6) & 63, points & 63
         mirror = c > 32
         a = jnp.where(mirror, (NG - a) & 63, a)
         b = jnp.where(mirror, (NG - b) & 63, b)
@@ -156,120 +218,36 @@
         picked = dot(y_part[...], chosen, ((1,), (0,)))
         picked = picked[0:2 * BOTH] + picked[2 * BOTH:]
         re0, re1, im0, im1 = (picked[i * PAIRS:(i + 1) * PAIRS] for i in range(4))
-        turns = jnp.concatenate([(a * x0) & 63, (a * (x0 + 1)) & 63], 1)
+        turns = jnp.concatenate([(a * (2 * f)) & 63, (a * (2 * f + 1)) & 63], 1)
         phase = dot(wx[...], (turn_row == turns).astype(F32), ((1,), (0,)), lax.Precision.HIGHEST)
-        cos0, cos1 = phase[0:1, 0:CHIP_POINTS], phase[0:1, CHIP_POINTS:]
-        sin0, sin1 = phase[1:2, 0:CHIP_POINTS], phase[1:2, CHIP_POINTS:]
+        cos0, cos1 = phase[0:1, 0:WIDE], phase[0:1, WIDE:]
+        sin0, sin1 = phase[1:2, 0:WIDE], phase[1:2, WIDE:]
         sign = jnp.where(mirror, -up, up)
         real = (cos0 * re0 + sin0 * im0 + cos1 * re1 + sin1 * im1) * up
         imag = (cos0 * im0 - sin0 * re0 + cos1 * im1 - sin1 * re1) * sign
         real, imag = jnp.floor(real + 0.5), jnp.floor(imag + 0.5)
-        middle_re, middle_im = real[:, 128:256], imag[:, 128:256]
-        for core in range(2):
-            if core == 0:
-                middle = jnp.where(half_lane, middle_re, pltpu.roll(middle_im, NG, 1))
-            else:
-                middle = jnp.where(half_lane, pltpu.roll(middle_re, NG, 1), middle_im)
-            lanes = slice(256 * core, 256 * core + 128)
-            slab = jnp.concatenate([real[:, lanes], imag[:, lanes], middle, level_rows], 0)
-            out[core, j] = slab.astype(jnp.int32).astype(jnp.int16)
-        return 0
-
-    lax.fori_loop(0, CHIPS, select, 0)
-
-
-def front(pair_c, pair_v, energy_c, energy_v, plane, psi_c, psi_v, g_index, total_pairs):
-    smem = pl.BlockSpec(memory_space=pltpu.SMEM)
-    vmem = pl.BlockSpec(memory_space=pltpu.VMEM)
-    anywhere = pl.BlockSpec(memory_space=pl.ANY)
-    return pl.pallas_call(
-        functools.partial(front_kernel, total_pairs),
-        out_shape=jax.ShapeDtypeStruct((2, CHIPS, 128, 128), jnp.int16),
-        in_specs=[smem] * 5 + [anywhere] * 2 + [vmem] * 4,
-        out_specs=vmem,
-        scratch_shapes=[
-            pltpu.VMEM(psi_v.shape, BF16),
-            pltpu.VMEM((PAIRS, NG, 128), BF16),
-            pltpu.VMEM((PAIRS * NG, 128), F32),
-            pltpu.VMEM((HALF_C, 128, 128), F32),
-            pltpu.VMEM((4 * BOTH, KEYS), BF16),
-            pltpu.SemaphoreType.DMA((2,)),
-        ],
-        compiler_params=pltpu.CompilerParams(vmem_limit_bytes=40 * 1024 * 1024),
-    )(
-        pair_c, pair_v, energy_c, energy_v, plane, psi_c, psi_v,
-        jnp.asarray(table_z()), jnp.asarray(table_y()), jnp.asarray(table_x()), g_index,
-    )
-
-
-def exchange_kernel(
-    q, chi_real, chi_imag,
-    core_in, chip_out, chip_in, block, z_blocks, row_blocks, col_blocks,
-    core_send, core_recv, chip_send, chip_recv, z_send, z_recv,
-    row_send, row_recv, plane_send, plane_recv, relay_send, relay_recv,
-):
-    f, g = lax.axis_index("fft"), lax.axis_index("grp")
-    core, chip, z = f % 2, f // 2, f // 4
-    x = chip % 2
-    sibling = f + 1 - 2 * core
-
-    def remote(src, dst, send, recv, to):
-        return pltpu.make_async_remote_copy(
-            src_ref=src, dst_ref=dst, send_sem=send, recv_sem=recv,
-            device_id=to, device_id_type=MESH,
-        )
-
-    barrier = pltpu.get_barrier_semaphore()
-    pl.semaphore_signal(barrier, 1, device_id=(sibling, g), device_id_type=MESH)
-
-    def greet_chip(k, _):
-        to = ((2 * chip + 2 * k) % 32 + core, g)
-        pl.semaphore_signal(barrier, 1, device_id=to, device_id_type=MESH)
-        return 0
-
-    lax.fori_loop(1, CHIPS, greet_chip, 0)
-
-    def greet_plane(k, _):
-        to = (z * 4 + (k % 2) * 2 + core, (g + k // 2) % 8)
-        pl.semaphore_signal(barrier, 1, device_id=to, device_id_type=MESH)
-        return 0
-
-    lax.fori_loop(2, 16, greet_plane, 0)
-    pl.semaphore_wait(barrier, 30)
-
-    def to_sibling(j):
-        return remote(q.at[1 - core, j], core_in.at[j], core_send.at[j], core_recv.at[j], (sibling, g))
-
-    def send_core(k, _):
-        to_sibling((chip + k) % CHIPS).start()
-        return 0
-
-    lax.fori_loop(1, CHIPS + 1, send_core, 0)
-
-    tail = lax.broadcasted_iota(jnp.int32, (128, 128), 0) >= 120
-
-    def to_chip(j):
-        return remote(
-            chip_out.at[j], chip_in.at[chip], chip_send.at[j], chip_recv.at[chip], (2 * j + core, g)
-        )
-
-    def add_core(k, _):
-        j = (chip + k) % CHIPS
-        to_sibling(j).wait_recv()
-        own, other = q[core, j].astype(jnp.int32).astype(F32), core_in[j].astype(jnp.int32).astype(F32)
-        own_level, other_level = own[120:121], other[120:121]
-        level = jnp.maximum(own_level, other_level) + 1.0
-        total = own * jnp.exp2(own_level - level) + other * jnp.exp2(other_level - level)
-        total = jnp.where(tail, level, jnp.floor(total + 0.5))
-        chip_out[j] = total.astype(jnp.int32).astype(jnp.int16)
-
-        @pl.when(k < CHIPS)
+        for n in range(2):
+            at = n * CHIP_POINTS
+            middle_re, middle_im = real[:, at + 128:at + 256], imag[:, at + 128:at + 256]
+            for side in range(2):
+                if side == 0:
+                    middle = jnp.where(half_lane, middle_re, pltpu.roll(middle_im, NG, 1))
+                else:
+                    middle = jnp.where(half_lane, pltpu.roll(middle_re, NG, 1), middle_im)
+                lanes = slice(at + 256 * side, at + 256 * side + 128)
+                slab = jnp.concatenate([real[:, lanes], imag[:, lanes], middle, level_rows], 0)
+                q[side, 2 * m + n] = slab.astype(jnp.int32).astype(jnp.int16)
+        for n in range(2):
+            to_sibling(2 * m + n).start()
+
+        @pl.when(k > 0)
         def _():
-            to_chip(j).start()
-
-        return 0
-
-    lax.fori_loop(1, CHIPS + 1, add_core, 0)
+            add_core(k - 1)
+
+        return 0
+
+    lax.fori_loop(0, 8, select, 0)
+    add_core(7)
 
     def scaled(slab):
         slab = slab.astype(jnp.int32).astype(F32)
@@ -429,32 +407,6 @@
     lax.fori_loop(0, 16, drain_plane, 0)
 
 
-def exchange(q, rows, columns):
-    vmem = pl.BlockSpec(memory_space=pltpu.VMEM)
-    dma = pltpu.SemaphoreType.DMA
-    slabs = pltpu.VMEM((CHIPS, 128, 128), jnp.int16)
-    blocks = pltpu.VMEM((8, 128, 128), BF16)
-    shape = jax.ShapeDtypeStruct((rows, columns), F32)
-    return pl.pallas_call(
-        exchange_kernel,
-        out_shape=(shape, shape),
-        in_specs=[vmem],
-        out_specs=(vmem, vmem),
-        scratch_shapes=[
-            slabs, slabs, slabs,
-            pltpu.VMEM((128, 128), BF16),
-            blocks, blocks,
-            pltpu.VMEM((2, 2, 8, 128, 128), BF16),
-            dma((CHIPS,)), dma((CHIPS,)), dma((CHIPS,)), dma((CHIPS,)),
-            dma((8,)), dma((8,)), dma((8,)), dma((8,)),
-            dma((8, 2)), dma((2, 8)), dma((2, 8)), dma((2, 8)),
-        ],
-        compiler_params=pltpu.CompilerParams(
-            collective_id=0, has_side_effects=True, vmem_limit_bytes=40 * 1024 * 1024
-        ),
-    )(q)
-
-
 def per_device(
     psi_valence,
     psi_conduction,
@@ -468,14 +420,46 @@
         bands = psi.shape[0]
         return psi.reshape(bands, 2, 32, 128).transpose(0, 2, 1, 3).reshape(bands, NG, 128)
 
-    plane = (2 * lax.axis_index("fft")).astype(jnp.int32).reshape(1)
-    slabs = front(
-        pair_conduction, pair_valence, energy_conduction, energy_valence, plane,
-        tiles(psi_conduction), tiles(psi_valence), g_index.reshape(1, -1),
-        PAIRS * lax.axis_size("grp"),
+    psi_c, psi_v = tiles(psi_conduction), tiles(psi_valence)
+    points = g_index.shape[0]
+    shape = jax.ShapeDtypeStruct(
+        (points // lax.axis_size("fft"), points // lax.axis_size("grp")), F32
     )
-    points = g_index.shape[0]
-    return exchange(slabs, points // lax.axis_size("fft"), points // lax.axis_size("grp"))
+    smem = pl.BlockSpec(memory_space=pltpu.SMEM)
+    vmem = pl.BlockSpec(memory_space=pltpu.VMEM)
+    anywhere = pl.BlockSpec(memory_space=pl.ANY)
+    dma = pltpu.SemaphoreType.DMA
+    slabs = pltpu.VMEM((CHIPS, 128, 128), jnp.int16)
+    blocks = pltpu.VMEM((8, 128, 128), BF16)
+    return pl.pallas_call(
+        functools.partial(kernel, PAIRS * lax.axis_size("grp")),
+        out_shape=(shape, shape),
+        in_specs=[smem] * 4 + [anywhere] * 2 + [vmem] * 4,
+        out_specs=(vmem, vmem),
+        scratch_shapes=[
+            pltpu.VMEM(psi_v.shape, BF16),
+            pltpu.VMEM(psi_c.shape, BF16),
+            pltpu.VMEM((PAIRS * NG, 128), F32),
+            pltpu.VMEM((HALF_C, 128, 128), F32),
+            pltpu.VMEM((4 * BOTH, KEYS), BF16),
+            pltpu.VMEM((2, CHIPS, 128, 128), jnp.int16),
+            slabs, slabs, slabs,
+            pltpu.VMEM((128, 128), BF16),
+            blocks, blocks,
+            pltpu.VMEM((2, 2, 8, 128, 128), BF16),
+            dma((2,)),
+            dma((CHIPS,)), dma((CHIPS,)), dma((CHIPS,)), dma((CHIPS,)),
+            dma((8,)), dma((8,)), dma((8,)), dma((8,)),
+            dma((8, 2)), dma((2, 8)), dma((2, 8)), dma((2, 8)),
+        ],
+        compiler_params=pltpu.CompilerParams(
+            collective_id=0, has_side_effects=True, vmem_limit_bytes=62 * 1024 * 1024
+        ),
+    )(
+        pair_conduction, pair_valence, energy_conduction, energy_valence, psi_c, psi_v,
+        jnp.asarray(table_z()), jnp.asarray(table_y()), jnp.asarray(table_x()),
+        g_index.reshape(1, -1),
+    )
 
 
 def solution(mesh):

time: 88.2 us -> 55.7 us (0.63); the launches traced: 86.7 us -> 55.1 us
  Pallas kernels: 74.7 us -> 50.6 us
  local copies, waits for them, and re-layouts: 11.3 us -> 3.83 us
    pallas_call x2 -> x1, Pallas kernels: 74.7 us -> 50.6 us  [per_device(): pl.pallas_call(functools.partial(kernel, PAIRS * lax.axis_size('grp')), o...]
    unnamed x22 -> x2, local copies, waits for them, and re-layouts: 11.3 us -> 3.83 us
where the time goes in v2:
time: 55.7 us; the launch traced here: 55.1 us
  Pallas kernels  50.6 us (91%)
  local copies, waits for them, and re-layouts  3.83 us (7%)
  between operations  0.64 us (1%)
    pallas_call x1, Pallas kernels, per_device(): pl.pallas_call(functools.partial(kernel, PAIRS * lax.axis_size('grp')), o...  50.6 us
    unnamed x2, local copies, waits for them, and re-layouts  3.83 us

profile of v2, /device:TPU:13, one launch (start us, length us, event | category | flops | bytes accessed | tf_op | source)
XLA Modules:
  0.0 55.1 jit_solution(16488713617735106089)
XLA Ops:
  0.6 50.6 %shard_map.113 = (f32[192,768]{1,0:T(8,128)}, f32[192,768]{1,0:T(8,128)}) custom-call(s32[40]{0:T(128)} %pair_c.1, s32[40]{0:T(128)} %pair_v.1, f32[384]{0:T(512)} %energy_c.1, f32[16]{0:T(128)} %energy_v.1, bf16[384,64,128]{2,1,0:T(8,128)(2,1)} %bitcast.11, bf16[16,64,128]{2,1,0:T(8,128)(2,1)} %bitcast.12, bf16[272,768]{1,0:T(8,128)(2,1)} %constant.6.clone.wz, ...), custom_call_target="tpu_custom_call" | custom-call | tf_op jit(solution)/shard_map/pallas_call | solution.py:434
  51.3 1.9 %copy.16 = f32[192,768]{1,0:T(8,128)} copy(f32[192,768]{1,0:T(8,128)} %get-tuple-element.4) | data formatting | bytes 1179648
  53.2 1.9 %copy.17 = f32[192,768]{1,0:T(8,128)} copy(f32[192,768]{1,0:T(8,128)} %get-tuple-element.5) | data formatting | bytes 1179648

commit v3 on v2

v3 whole, which is shorter than its diff:
```python
import functools
import math

import jax
import jax.numpy as jnp
import ml_dtypes
import numpy as np
from jax import lax
from jax.experimental import pallas as pl
from jax.experimental.pallas import tpu as pltpu
from jax.sharding import PartitionSpec as P

NG = 64
HALF_C = 34
KEYS = HALF_C * NG
PAIRS = 40
BOTH = 2 * PAIRS
CHIPS = 16
CHIP_POINTS = 384
WIDE = 512
FULL, MIDDLE = 80, 48
BF16 = jnp.bfloat16
F32 = jnp.float32
FP8 = jnp.float8_e4m3fn
MESH = pl.DeviceIdType.MESH


def split_table(table):
    high = table.astype(ml_dtypes.bfloat16)
    low = (table - high.astype(np.float64)).astype(ml_dtypes.bfloat16)
    return high, low


def table_z():
    c, z = np.arange(33)[:, None], np.arange(NG)[None, :]
    angle = 2 * np.pi * ((c * z) % NG) / NG
    table = np.zeros((HALF_C, 4, 2, 4, NG))
    for y in range(4):
        table[:33, y, 0, y] = np.cos(angle)
        table[:33, y, 1, y] = -np.sin(angle)
    high, low = split_table(table.reshape(HALF_C * 8, 4 * NG))
    return np.concatenate([high, high, low], 1)


def table_y():
    y, b = np.arange(NG)[:, None], np.arange(NG)[None, :]
    angle = 2 * np.pi * ((y * b) % NG) / NG
    table = np.zeros((NG, 2, 2, NG))
    table[:, 0, 0], table[:, 0, 1] = np.cos(angle), -np.sin(angle)
    table[:, 1, 0], table[:, 1, 1] = np.sin(angle), np.cos(angle)
    high, low = split_table(table.reshape(2 * NG, 2 * NG))
    return np.concatenate([high, high, low], 0)


def table_x():
    angle = 2 * np.pi * np.arange(NG) / NG
    table = np.zeros((8, NG), np.float32)
    table[0], table[1] = np.cos(angle), np.sin(angle)
    return table


def split(x):
    high = x.astype(BF16)
    return high, (x - high.astype(F32)).astype(BF16)


def dot(a, b, contract, precision=None):
    return lax.dot_general(
        a, b, (contract, ((), ())), precision=precision, preferred_element_type=F32
    )


def kernel(
    total_pairs,
    pair_c, pair_v, energy_c, energy_v,
    psi_c, psi_v, wz, wy, wx, g_index,
    chi_real, chi_imag,
    band_v, band_c, density, z_part, y_part, bounds, scales,
    own1, own2, core_in1, core_in2, chip_out1, chip_out2, chip_in1, chip_in2,
    block1, block2, z_blocks1, z_blocks2, row_blocks1, row_blocks2, col_blocks1, col_blocks2,
    load, bound_send, bound_recv, scale_send, scale_recv,
    core_send, core_recv, chip_send, chip_recv, z_send, z_recv,
    row_send, row_recv, plane_send, plane_recv, relay_send, relay_recv,
):
    own, core_in = (own1, own2), (core_in1, core_in2)
    chip_out, chip_in = (chip_out1, chip_out2), (chip_in1, chip_in2)
    block, z_blocks = (block1, block2), (z_blocks1, z_blocks2)
    row_blocks, col_blocks = (row_blocks1, row_blocks2), (col_blocks1, col_blocks2)
    f, g = lax.axis_index("fft"), lax.axis_index("grp")
    core, chip, z = f % 2, f // 2, f // 4
    x = chip % 2
    sibling = f + 1 - 2 * core

    copy_c = pltpu.make_async_copy(psi_c, band_c, load.at[0])
    copy_v = pltpu.make_async_copy(psi_v, band_v, load.at[1])
    copy_c.start()
    copy_v.start()

    def remote(src, dst, send, recv, to):
        return pltpu.make_async_remote_copy(
            src_ref=src, dst_ref=dst, send_sem=send, recv_sem=recv,
            device_id=to, device_id_type=MESH,
        )

    barrier = pltpu.get_barrier_semaphore()
    pl.semaphore_signal(barrier, 1, device_id=(sibling, g), device_id_type=MESH)

    def greet_chip(k, _):
        to = ((2 * chip + 2 * k) % 32 + core, g)
        pl.semaphore_signal(barrier, 1, device_id=to, device_id_type=MESH)
        return 0

    lax.fori_loop(1, CHIPS, greet_chip, 0)

    def greet_plane(k, _):
        to = (z * 4 + (k % 2) * 2 + core, (g + k // 2) % 8)
        pl.semaphore_signal(barrier, 1, device_id=to, device_id_type=MESH)
        return 0

    lax.fori_loop(2, 16, greet_plane, 0)

    column = lax.broadcasted_iota(jnp.int32, (8, BOTH), 1)
    column = jnp.where(column >= PAIRS, column - PAIRS, column)

    def gaps(p, gap):
        return jnp.where(column == p, energy_c[pair_c[p]] - energy_v[pair_v[p]], gap)

    gap = lax.fori_loop(0, PAIRS, gaps, jnp.ones((8, BOTH), F32))
    factor = jnp.sqrt(2.0 / gap) * (total_pairs ** (-0.25) * NG ** (-1.5))

    copy_v.wait()
    copy_c.wait()

    def multiply(p, _):
        start = pl.multiple_of(p * NG, NG)
        density[pl.ds(start, NG), :] = (
            band_v[pair_v[p]].astype(F32) * band_c[pair_c[p]].astype(F32)
        )
        return 0

    lax.fori_loop(0, PAIRS, multiply, 0)

    def along_z(i, size):
        lines = []
        for t in range(2):
            lines.append(jnp.concatenate([
                density[pl.ds(4 * i + 2 * t + n, PAIRS, stride=NG), :] for n in range(2)
            ], 0))
        high, low = split(jnp.concatenate(lines, 1))
        lines = jnp.concatenate([high, low, high], 1)
        result = dot(wz[...], lines, ((1,), (1,))).reshape(HALF_C, 8, BOTH) * factor
        start = pl.multiple_of(8 * i, 8)
        z_part[:, pl.ds(start, 8), 0:BOTH] = result
        return size + jnp.abs(result)

    size = lax.fori_loop(
        0, NG // 4, along_z, jnp.zeros((HALF_C, 8, BOTH), F32), unroll=8
    )
    size = jnp.max(jnp.sum(size, 1), 0, keepdims=True)
    most = jnp.maximum(jnp.max(size, 1, keepdims=True), 1e-30)
    size = jnp.max(size[:, 0:PAIRS] + size[:, PAIRS:], 1, keepdims=True)
    bounds[core] = jnp.broadcast_to(jnp.maximum(size, 1e-30), (8, 128))
    fit = 400.0 / most

    pl.semaphore_wait(barrier, 30)
    swap = remote(bounds.at[core], bounds.at[core], bound_send.at[0], bound_recv.at[0], (sibling, g))
    swap.start()

    lane = lax.broadcasted_iota(jnp.int32, (BOTH, 128), 1)

    def along_y(k, _):
        lines = jnp.concatenate([z_part[2 * k + n].T[0:BOTH] for n in range(2)], 0)
        high, low = split(lines)
        result = dot(jnp.concatenate([high, low, high], 1), wy[...], ((1,), (0,)))
        first, second = result[0:BOTH], result[BOTH:]
        real = jnp.where(lane < NG, first, pltpu.roll(second, NG, 1))
        imag = jnp.where(lane < NG, pltpu.roll(first, NG, 1), second)
        rest = jnp.concatenate([real, imag], 0) * fit
        start = pl.multiple_of(128 * k, 128)
        for i in range(3):
            piece = rest.astype(FP8)
            y_part[2 * BOTH * i:2 * BOTH * (i + 1), pl.ds(start, 128)] = piece
            rest = rest - piece.astype(F32)
        return 0

    lax.fori_loop(0, HALF_C // 2, along_y, 0, unroll=HALF_C // 2)

    swap.wait_recv()
    bound = (bounds[0] + bounds[1]) * 1.001
    scales[chip] = bound * (1.0 / 32767.0)
    up = (32767.0 / fit) / bound[0:1, 0:1]

    def to_scale(j):
        return remote(
            scales.at[chip], scales.at[chip], scale_send.at[j], scale_recv.at[chip], (2 * j + core, g)
        )

    def send_scale(k, _):
        to_scale((chip + k) % CHIPS).start()
        return 0

    lax.fori_loop(1, CHIPS, send_scale, 0)

    half_lane = lax.broadcasted_iota(jnp.int32, (PAIRS, 128), 1) < NG
    key_row = lax.broadcasted_iota(jnp.int16, (KEYS, WIDE), 0)
    turn_row = lax.broadcasted_iota(jnp.int32, (NG, 2 * WIDE), 0)

    def to_sibling(h, j):
        return remote(
            own[h].at[1 - core, j], core_in[h].at[j], core_send.at[h, j], core_recv.at[h, j], (sibling, g)
        )

    def to_chip(h, j):
        return remote(
            chip_out[h].at[j], chip_in[h].at[chip],
            chip_send.at[h, j], chip_recv.at[h, chip], (2 * j + core, g),
        )

    def layer_of(k):
        return (z + (4 - (k + 1) // 2) * (2 * (k % 2) - 1) + 8) % 8

    def chips_of(h, k):
        layers = (k,) if h == 0 else (2 * k, 2 * k + 1)
        return [2 * layer_of(i) + n for i in layers for n in range(2)]

    def add_core(h, k):
        for j in chips_of(h, k):
            total = jnp.floor(own[h][core, j] + core_in[h][j] + 0.5).astype(jnp.int32)
            if h == 1:
                total = jnp.concatenate([total, jnp.zeros((MIDDLE - PAIRS, 128), jnp.int32)], 0)
            chip_out[h][j] = total.astype(jnp.int16)

    def arrive(h, k):
        for j in chips_of(h, k):
            to_sibling(h, j).wait_recv()

    def send(h, k, last):
        for j in chips_of(h, k):
            if last:
                @pl.when(j != chip)
                def _():
                    to_chip(h, j).start()
            else:
                to_chip(h, j).start()

    def select(h, k):
        chips = chips_of(h, k)
        tiles = [(j, t) for j in chips for t in ((0, 2) if h == 0 else (1,))]
        points = jnp.concatenate([
            g_index[0:1, pl.ds(pl.multiple_of(j * CHIP_POINTS + t * 128, 128), 128)]
            for j, t in tiles
        ], 1)
        a, b, c = points >> 12, (points >> 6) & 63, points & 63
        mirror = c > 32
        a = jnp.where(mirror, (NG - a) & 63, a)
        b = jnp.where(mirror, (NG - b) & 63, b)
        c = jnp.where(mirror, NG - c, c)
        key = (c * NG + b).astype(jnp.int16)
        chosen = jnp.where(key_row == key, BF16(1), BF16(0)).astype(FP8)
        picked = dot(y_part[...], chosen, ((1,), (0,)))
        picked = picked[0:2 * BOTH] + (picked[2 * BOTH:4 * BOTH] + picked[4 * BOTH:])
        re0, re1, im0, im1 = (picked[i * PAIRS:(i + 1) * PAIRS] for i in range(4))
        turns = jnp.concatenate([(a * (2 * f)) & 63, (a * (2 * f + 1)) & 63], 1)
        phase = dot(wx[...], (turn_row == turns).astype(F32), ((1,), (0,)), lax.Precision.HIGHEST)
        phase = phase * up
        cos0, cos1 = phase[0:1, 0:WIDE], phase[0:1, WIDE:]
        sin0, sin1 = phase[1:2, 0:WIDE], phase[1:2, WIDE:]
        real = cos0 * re0 + sin0 * im0 + cos1 * re1 + sin1 * im1
        imag = cos0 * im0 - sin0 * re0 + cos1 * im1 - sin1 * re1
        imag = jnp.where(mirror, -imag, imag)
        for n, (j, t) in enumerate(tiles):
            re, im = real[:, 128 * n:128 * (n + 1)], imag[:, 128 * n:128 * (n + 1)]
            if h == 0:
                own1[t // 2, j] = jnp.concatenate([re, im], 0)
            else:
                own2[0, j] = jnp.where(half_lane, re, pltpu.roll(im, NG, 1))
                own2[1, j] = jnp.where(half_lane, pltpu.roll(re, NG, 1), im)
        return chips

    def hand_over(h, chips):
        for j in chips:
            to_sibling(h, j).start()

    def step(h, k, added=None):
        if added is not None:
            arrive(*added)
        chips = select(h, k)
        if added is not None:
            add_core(*added)
        hand_over(h, chips)
        if added is not None:
            send(*added, False)

    def loop(first, last, body):
        def run(k, _):
            body(k)
            return 0
        lax.fori_loop(first, last, run, 0)

    loop(0, 2, lambda k: step(0, k))
    loop(2, 8, lambda k: step(0, k, (0, k - 2)))
    arrive(0, 6)
    chips = select(1, 0)
    add_core(0, 6)
    hand_over(1, chips)
    send(0, 6, False)
    arrive(0, 7)
    chips = select(1, 1)
    add_core(0, 7)
    hand_over(1, chips)
    send(0, 7, True)
    loop(2, 4, lambda k: step(1, k, (1, k - 2)))
    for k in (2, 3):
        arrive(1, k)
        add_core(1, k)
        send(1, k, k == 3)

    def scale_arrives(k):
        j = (chip + k) % CHIPS
        remote(
            scales.at[j], scales.at[j], scale_send.at[j], scale_recv.at[j], (2 * j + core, g)
        ).wait_recv()

    loop(1, CHIPS, scale_arrives)

    def to_z(h, k):
        other = (z + k) % 8
        return remote(
            block[h], z_blocks[h].at[z], z_send.at[h, other], z_recv.at[h, z],
            (other * 4 + x * 2 + core, g),
        )

    def to_row(h, k):
        other = (g + k) % 8
        return remote(
            block[h], row_blocks[h].at[g], row_send.at[h, other], row_recv.at[h, g], (f, other)
        )

    def near(k):
        return (k + 1) // 2 * (1 - 2 * (k % 2)) + 8

    for h in range(2):
        chip_in[h][chip] = chip_out[h][chip]

        def add_layer(k, total):
            layer = (2 * z - layer_of(k) + 8) % 8
            for n in range(2):
                j = 2 * layer + n

                @pl.when(j != chip)
                def _():
                    remote(
                        chip_out[h].at[j], chip_in[h].at[j],
                        chip_send.at[h, j], chip_recv.at[h, j], (2 * j + core, g),
                    ).wait_recv()

                total = total + chip_in[h][j].astype(jnp.int32).astype(F32) * scales[j, 0:1]
            return total

        total = lax.fori_loop(0, 8, add_layer, jnp.zeros(block[h].shape, F32))
        block[h][...] = total.astype(BF16)
        loop(1, 8, lambda k: to_z(h, near(k)).start())
        loop(1, 8, lambda k: to_row(h, k).start())
        z_blocks[h][z] = block[h][...]
        row_blocks[h][g] = block[h][...]

    def to_plane(h, layer, to_x):
        return remote(
            z_blocks[h].at[layer], col_blocks[h].at[core, x, g],
            plane_send.at[h, layer, to_x], plane_recv.at[h, x, g],
            (z * 4 + to_x * 2 + core, layer),
        )

    def stays(layer, to_x):
        return jnp.logical_and(layer == g, to_x == x)

    for h in range(2):
        def spread(k):
            layer = (z + near(k)) % 8

            @pl.when(k > 0)
            def _():
                remote(
                    block[h], z_blocks[h].at[layer], z_send.at[h, layer], z_recv.at[h, layer],
                    (layer * 4 + x * 2 + core, g),
                ).wait_recv()

            for to_x in range(2):
                @pl.when(stays(layer, to_x))
                def _():
                    col_blocks[h][core, x, g] = z_blocks[h][layer]

                @pl.when(jnp.logical_not(stays(layer, to_x)))
                def _():
                    to_plane(h, layer, to_x).start()

        loop(0, 8, spread)

    def relay(h, side, from_x, from_g):
        return remote(
            col_blocks[h].at[side, from_x, from_g], col_blocks[h].at[side, from_x, from_g],
            relay_send.at[h, from_x, from_g], relay_recv.at[h, from_x, from_g], (sibling, g),
        )

    for h in range(2):
        def pass_on(k):
            from_x, from_g = (x + k) % 2, (g + k // 2) % 8

            @pl.when(k > 0)
            def _():
                remote(
                    z_blocks[h].at[0], col_blocks[h].at[core, from_x, from_g],
                    plane_send.at[h, 0, 0], plane_recv.at[h, from_x, from_g],
                    (z * 4 + from_x * 2 + core, from_g),
                ).wait_recv()

            relay(h, core, from_x, from_g).start()

        loop(0, 16, pass_on)

    for h in range(2):
        def row_arrives(k):
            other = (g + k) % 8
            remote(
                block[h], row_blocks[h].at[other], row_send.at[h, other], row_recv.at[h, other], (f, other)
            ).wait_recv()

        loop(1, 8, row_arrives)
        loop(0, 16, lambda k: relay(h, 1 - core, k % 2, k // 2).wait_recv())

    half_wide = lax.broadcasted_iota(jnp.int32, (8 * PAIRS, 128), 1) < NG

    def gather(read1, read2):
        blocks1 = [read1(i).astype(F32) for i in range(8)]
        blocks2 = [read2(i).astype(F32) for i in range(8)]
        return (
            jnp.concatenate([b[0:PAIRS] for b in blocks1], 0),
            jnp.concatenate([b[PAIRS:] for b in blocks1], 0),
            jnp.concatenate([b[0:PAIRS] for b in blocks2], 0),
        )

    real, imag, middle = gather(lambda i: row_blocks1[i], lambda i: row_blocks2[i])
    full = jnp.concatenate([real, imag], 0).astype(BF16)
    half = jnp.concatenate([middle, pltpu.roll(middle, NG, 1)], 0)[:, 0:NG].astype(BF16)
    full_row = pl.multiple_of(core * NG, NG)
    half_row = pl.multiple_of((1 - core) * 128, NG)
    for side in range(2):
        real0, imag0, middle0 = gather(
            lambda i: col_blocks1[0, side, i], lambda i: col_blocks2[0, side, i]
        )
        real2, imag2, middle2 = gather(
            lambda i: col_blocks1[1, side, i], lambda i: col_blocks2[1, side, i]
        )
        real1 = jnp.where(half_wide, middle0, pltpu.roll(middle2, NG, 1))
        imag1 = jnp.where(half_wide, pltpu.roll(middle0, NG, 1), middle2)
        real = jnp.concatenate([real0, real1, real2], 1)
        imag = jnp.concatenate([imag0, imag1, imag2], 1)
        right_sum = jnp.concatenate([real, imag], 0).astype(BF16)
        right_cross = jnp.concatenate([imag, -real], 0).astype(BF16)
        lanes = slice(side * CHIP_POINTS, (side + 1) * CHIP_POINTS)
        for left, rows in ((full, pl.ds(full_row, 128)), (half, pl.ds(half_row, NG))):
            chi_real[rows, lanes] = -dot(left, right_sum, ((0,), (0,)))
            chi_imag[rows, lanes] = dot(left, right_cross, ((0,), (0,)))

    swap.wait_send()

    def drain_chips(k):
        to_scale((chip + k) % CHIPS).wait_send()
        for h in range(2):
            to_chip(h, (chip + k) % CHIPS).wait_send()

    loop(1, CHIPS, drain_chips)

    def drain_blocks(k):
        for h in range(2):
            to_z(h, k).wait_send()
            to_row(h, k).wait_send()

    loop(1, 8, drain_blocks)

    def drain_plane(k):
        for h in range(2):
            to_sibling(h, k).wait_send()

            @pl.when(jnp.logical_not(stays(k // 2, k % 2)))
            def _():
                to_plane(h, k // 2, k % 2).wait_send()

            relay(h, core, k % 2, k // 2).wait_send()

    loop(0, 16, drain_plane)


def per_device(
    psi_valence,
    psi_conduction,
    energy_valence,
    energy_conduction,
    pair_valence,
    pair_conduction,
    g_index,
):
    def tiles(psi):
        bands = psi.shape[0]
        return psi.reshape(bands, 2, 32, 128).transpose(0, 2, 1, 3).reshape(bands, NG, 128)

    psi_c, psi_v = tiles(psi_conduction), tiles(psi_valence)
    points = g_index.shape[0]
    shape = jax.ShapeDtypeStruct(
        (points // lax.axis_size("fft"), points // lax.axis_size("grp")), F32
    )
    smem = pl.BlockSpec(memory_space=pltpu.SMEM)
    vmem = pl.BlockSpec(memory_space=pltpu.VMEM)
    anywhere = pl.BlockSpec(memory_space=pl.ANY)
    dma = pltpu.SemaphoreType.DMA

    def both(dtype, *lead):
        return [pltpu.VMEM((*lead, rows, 128), dtype) for rows in (FULL, MIDDLE)]

    return pl.pallas_call(
        functools.partial(kernel, PAIRS * lax.axis_size("grp")),
        out_shape=(shape, shape),
        in_specs=[smem] * 4 + [anywhere] * 2 + [vmem] * 4,
        out_specs=(vmem, vmem),
        scratch_shapes=[
            pltpu.VMEM(psi_v.shape, BF16),
            pltpu.VMEM(psi_c.shape, BF16),
            pltpu.VMEM((PAIRS * NG, 128), F32),
            pltpu.VMEM((HALF_C, 128, 128), F32),
            pltpu.VMEM((6 * BOTH, KEYS), FP8),
            pltpu.VMEM((2, 8, 128), F32),
            pltpu.VMEM((CHIPS, 8, 128), F32),
            pltpu.VMEM((2, CHIPS, FULL, 128), F32), pltpu.VMEM((2, CHIPS, PAIRS, 128), F32),
            pltpu.VMEM((CHIPS, FULL, 128), F32), pltpu.VMEM((CHIPS, PAIRS, 128), F32),
            *both(jnp.int16, CHIPS), *both(jnp.int16, CHIPS),
            *both(BF16), *both(BF16, 8), *both(BF16, 8), *both(BF16, 2, 2, 8),
            dma((2,)), dma((1,)), dma((1,)), dma((CHIPS,)), dma((CHIPS,)),
            dma((2, CHIPS)), dma((2, CHIPS)), dma((2, CHIPS)), dma((2, CHIPS)),
            dma((2, 8)), dma((2, 8)), dma((2, 8)), dma((2, 8)),
            dma((2, 8, 2)), dma((2, 2, 8)), dma((2, 2, 8)), dma((2, 2, 8)),
        ],
        compiler_params=pltpu.CompilerParams(
            collective_id=0, has_side_effects=True, vmem_limit_bytes=62 * 1024 * 1024
        ),
    )(
        pair_conduction, pair_valence, energy_conduction, energy_valence, psi_c, psi_v,
        jnp.asarray(table_z()), jnp.asarray(table_y()), jnp.asarray(table_x()),
        g_index.reshape(1, -1),
    )


def solution(mesh):
    placed = (P(None, "fft", None), P(None, "fft", None), P(), P(), P("grp"), P("grp"), P())
    return jax.shard_map(
        per_device,
        mesh=mesh,
        in_specs=placed,
        out_specs=(P("fft", "grp"), P("fft", "grp")),
        check_vma=False,
    )
```

time: 55.7 us -> 55.6 us (level)
  the two profiles are of different devices: /device:TPU:13 before, /device:TPU:1 now
where the time goes in v3:
time: 55.6 us; the launch traced here: 55.4 us
  Pallas kernels  50.9 us (92%)
  local copies, waits for them, and re-layouts  3.83 us (7%)
  between operations  0.64 us (1%)
    pallas_call x1, Pallas kernels, per_device(): pl.pallas_call(functools.partial(kernel, PAIRS * lax.axis_size('grp')), o...  50.9 us
    unnamed x2, local copies, waits for them, and re-layouts  3.83 us

profile of v3, /device:TPU:1, one launch (start us, length us, event | category | flops | bytes accessed | tf_op | source)
XLA Modules:
  0.0 55.4 jit_solution(5929567742207988285)
XLA Ops:
  0.6 50.9 %shard_map.113 = (f32[192,768]{1,0:T(8,128)}, f32[192,768]{1,0:T(8,128)}) custom-call(s32[40]{0:T(128)} %pair_c.1, s32[40]{0:T(128)} %pair_v.1, f32[384]{0:T(512)} %energy_c.1, f32[16]{0:T(128)} %energy_v.1, bf16[384,64,128]{2,1,0:T(8,128)(2,1)} %bitcast.11, bf16[16,64,128]{2,1,0:T(8,128)(2,1)} %bitcast.12, bf16[272,768]{1,0:T(8,128)(2,1)} %constant.6.clone.wz, ...), custom_call_target="tpu_custom_call" | custom-call | tf_op jit(solution)/shard_map/pallas_call | solution.py:520
  51.6 1.9 %copy.16 = f32[192,768]{1,0:T(8,128)} copy(f32[192,768]{1,0:T(8,128)} %get-tuple-element.4) | data formatting | bytes 1179648
  53.5 1.9 %copy.17 = f32[192,768]{1,0:T(8,128)} copy(f32[192,768]{1,0:T(8,128)} %get-tuple-element.5) | data formatting | bytes 1179648

commit v4 on v2

v4 whole, which is shorter than its diff:
```python
import functools
import math

import jax
import jax.numpy as jnp
import ml_dtypes
import numpy as np
from jax import lax
from jax.experimental import pallas as pl
from jax.experimental.pallas import tpu as pltpu
from jax.sharding import PartitionSpec as P

NG = 64
HALF_C = 34
KEYS = HALF_C * NG
PAIRS = 40
BOTH = 2 * PAIRS
CHIPS = 16
LOADS = 4
PIECE = NG // LOADS
CHIP_POINTS = 384
WIDE = 2 * CHIP_POINTS
BF16 = jnp.bfloat16
F32 = jnp.float32
FP8 = jnp.float8_e4m3fn
MESH = pl.DeviceIdType.MESH


def split_table(table):
    high = table.astype(ml_dtypes.bfloat16)
    low = (table - high.astype(np.float64)).astype(ml_dtypes.bfloat16)
    return high, low


def table_z():
    c, z = np.arange(33)[:, None], np.arange(NG)[None, :]
    angle = 2 * np.pi * ((c * z) % NG) / NG
    table = np.zeros((HALF_C, 4, 2, 4, NG))
    for y in range(4):
        table[:33, y, 0, y] = np.cos(angle)
        table[:33, y, 1, y] = -np.sin(angle)
    high, low = split_table(table.reshape(HALF_C * 8, 4 * NG))
    return np.concatenate([high, high, low], 1)


def table_y():
    y, b = np.arange(NG)[:, None], np.arange(NG)[None, :]
    angle = 2 * np.pi * ((y * b) % NG) / NG
    table = np.zeros((NG, 2, 2, NG))
    table[:, 0, 0], table[:, 0, 1] = np.cos(angle), -np.sin(angle)
    table[:, 1, 0], table[:, 1, 1] = np.sin(angle), np.cos(angle)
    high, low = split_table(table.reshape(2 * NG, 2 * NG))
    return np.concatenate([high, high, low], 0)


def table_x():
    angle = 2 * np.pi * np.arange(NG) / NG
    table = np.zeros((16, NG), ml_dtypes.bfloat16)
    for row, rest in ((0, np.cos(angle)), (3, np.sin(angle))):
        for i in range(3):
            table[row + i] = rest.astype(ml_dtypes.bfloat16)
            rest = rest - table[row + i].astype(np.float64)
    return table


def split(x):
    high = x.astype(BF16)
    return high, (x - high.astype(F32)).astype(BF16)


def dot(a, b, contract, precision=None):
    return lax.dot_general(
        a, b, (contract, ((), ())), precision=precision, preferred_element_type=F32
    )


def kernel(
    total_pairs,
    pair_c, pair_v, energy_c, energy_v,
    psi_c, psi_v, wz, wy, wx, g_index,
    rows_out, columns_out,
    band_v, band_c0, band_c1, band_c2, band_c3, density, z_part, y_part, point_data,
    own, core_in, chip_out, chip_in, block, z_blocks, row_blocks, col_blocks, load,
    core_send, core_recv, chip_send, chip_recv, z_send, z_recv,
    row_send, row_recv, plane_send, plane_recv, relay_send, relay_recv,
):
    f, g = lax.axis_index("fft"), lax.axis_index("grp")
    core, chip, z = f % 2, f // 2, f // 4
    x = chip % 2
    sibling = f + 1 - 2 * core
    partner = chip + 1 - 2 * x

    band_c = (band_c0, band_c1, band_c2, band_c3)

    def piece(i):
        rows = pl.ds(i * PIECE, PIECE)
        return pltpu.make_async_copy(psi_c.at[:, rows], band_c[i], load.at[8 + i])

    copy_v = pltpu.make_async_copy(psi_v, band_v, load.at[1])
    copy_v.start()
    for i in range(LOADS):
        piece(i).start()

    stores = [
        pltpu.make_async_copy(row_blocks, rows_out, load.at[2]),
        pltpu.make_async_copy(col_blocks.at[core], columns_out.at[core], load.at[3]),
        pltpu.make_async_copy(col_blocks.at[1 - core], columns_out.at[1 - core], load.at[4]),
    ]

    def remote(src, dst, send, recv, to):
        return pltpu.make_async_remote_copy(
            src_ref=src, dst_ref=dst, send_sem=send, recv_sem=recv,
            device_id=to, device_id_type=MESH,
        )

    barrier = pltpu.get_barrier_semaphore()
    pl.semaphore_signal(barrier, 1, device_id=(sibling, g), device_id_type=MESH)

    def greet_chip(k, _):
        to = ((2 * chip + 2 * k) % 32 + core, g)
        pl.semaphore_signal(barrier, 1, device_id=to, device_id_type=MESH)
        return 0

    lax.fori_loop(1, CHIPS, greet_chip, 0)

    def greet_plane(k, _):
        to = (z * 4 + (k % 2) * 2 + core, (g + k // 2) % 8)
        pl.semaphore_signal(barrier, 1, device_id=to, device_id_type=MESH)
        return 0

    lax.fori_loop(2, 16, greet_plane, 0)

    turn_row = lax.broadcasted_iota(jnp.int32, (NG, 2 * CHIP_POINTS), 0)

    def prepare(j, _):
        lanes = pl.ds(pl.multiple_of(j * CHIP_POINTS, 128), CHIP_POINTS)
        points = g_index[0:1, lanes]
        a, b, c = points >> 12, (points >> 6) & 63, points & 63
        mirror = c > 32
        a = jnp.where(mirror, (NG - a) & 63, a)
        b = jnp.where(mirror, (NG - b) & 63, b)
        c = jnp.where(mirror, NG - c, c)
        turns = jnp.concatenate([(a * (2 * f)) & 63, (a * (2 * f + 1)) & 63], 1)
        phase = dot(wx[...], jnp.where(turn_row == turns, BF16(1), BF16(0)), ((1,), (0,)))
        cos = phase[0:1] + (phase[1:2] + phase[2:3])
        sin = phase[3:4] + (phase[4:5] + phase[5:6])
        sign = jnp.where(mirror, -1.0, 1.0)
        first, second = slice(0, CHIP_POINTS), slice(CHIP_POINTS, 2 * CHIP_POINTS)
        point_data[:, lanes] = jnp.concatenate([
            cos[:, first], sin[:, first], cos[:, second], sin[:, second],
            sign, (c * NG + b).astype(F32), sign, sign,
        ], 0)
        return 0

    lax.fori_loop(0, CHIPS, prepare, 0)

    column = lax.broadcasted_iota(jnp.int32, (8, BOTH), 1)
    column = jnp.where(column >= PAIRS, column - PAIRS, column)

    def gaps(p, gap):
        return jnp.where(column == p, energy_c[pair_c[p]] - energy_v[pair_v[p]], gap)

    gap = lax.fori_loop(0, PAIRS, gaps, jnp.ones((8, BOTH), F32))
    factor = jnp.sqrt(2.0 / gap) * (total_pairs ** (-0.25) * NG ** (-1.5))

    copy_v.wait()

    def along_z(i, size):
        lines = []
        for t in range(2):
            lines.append(jnp.concatenate([
                density[pl.ds(4 * i + 2 * t + n, PAIRS, stride=NG), :] for n in range(2)
            ], 0))
        high, low = split(jnp.concatenate(lines, 1))
        lines = jnp.concatenate([high, low, high], 1)
        result = dot(wz[...], lines, ((1,), (1,))).reshape(HALF_C, 8, BOTH) * factor
        start = pl.multiple_of(8 * i, 8)
        z_part[:, pl.ds(start, 8), 0:BOTH] = result
        return size + jnp.abs(result)

    size = jnp.zeros((HALF_C, 8, BOTH), F32)
    for part in range(LOADS):
        piece(part).wait()

        def multiply(p, _):
            rows = pl.ds(part * PIECE, PIECE)
            start = pl.multiple_of(p * NG + part * PIECE, PIECE)
            density[pl.ds(start, PIECE), :] = (
                band_v[pair_v[p], rows].astype(F32) * band_c[part][pair_c[p]].astype(F32)
            )
            return 0

        lax.fori_loop(0, PAIRS, multiply, 0, unroll=4)
        for i in range(PIECE // 4):
            size = along_z(part * (PIECE // 4) + i, size)

    size = jnp.max(jnp.sum(size, 1), 0, keepdims=True)
    most = jnp.maximum(jnp.max(size, 1, keepdims=True), 1e-30)
    size = jnp.max(size[:, 0:PAIRS] + size[:, PAIRS:], 1, keepdims=True)
    bound_rows = jnp.broadcast_to(jnp.maximum(size, 1e-30), (8, 128))
    fit = 400.0 / most

    lane = lax.broadcasted_iota(jnp.int32, (BOTH, 128), 1)

    def along_y(k, _):
        lines = jnp.concatenate([z_part[2 * k + n].T[0:BOTH] for n in range(2)], 0)
        high, low = split(lines)
        result = dot(jnp.concatenate([high, low, high], 1), wy[...], ((1,), (0,)))
        first, second = result[0:BOTH], result[BOTH:]
        real = jnp.where(lane < NG, first, pltpu.roll(second, NG, 1))
        imag = jnp.where(lane < NG, pltpu.roll(first, NG, 1), second)
        rest = jnp.concatenate([real, imag], 0) * fit
        start = pl.multiple_of(128 * k, 128)
        for i in range(3):
            piece = rest.astype(FP8)
            y_part[2 * BOTH * i:2 * BOTH * (i + 1), pl.ds(start, 128)] = piece
            rest = rest - piece.astype(F32)
        return 0

    lax.fori_loop(0, HALF_C // 2, along_y, 0, unroll=HALF_C // 2)

    half_lane = lax.broadcasted_iota(jnp.int32, (PAIRS, 128), 1) < NG
    key_row = lax.broadcasted_iota(jnp.int16, (KEYS, WIDE), 0)
    tail = lax.broadcasted_iota(jnp.int32, (128, 128), 0) >= 120
    unfit = most / 400.0

    pl.semaphore_wait(barrier, 30)

    def to_sibling(j):
        return remote(
            own.at[1 - core, j], core_in.at[j], core_send.at[j], core_recv.at[j], (sibling, g)
        )

    def to_chip(j):
        return remote(
            chip_out.at[j], chip_in.at[chip], chip_send.at[j], chip_recv.at[chip], (2 * j + core, g)
        )

    def layer_of(k):
        return (z + (4 - (k + 1) // 2) * (2 * (k % 2) - 1) + 8) % 8

    def arrive(k):
        for n in range(2):
            to_sibling(2 * layer_of(k) + n).wait_recv()

    def add_core(k):
        for n in range(2):
            j = 2 * layer_of(k) + n
            total = own[core, j] + core_in[j]
            level = jnp.floor(jnp.log2(total[120:121] * 1.001)) + 1.0
            total = jnp.where(tail, level, jnp.floor(total * jnp.exp2(15.0 - level) + 0.5))
            chip_out[j] = total.astype(jnp.int32).astype(jnp.int16)

    def select(k):
        m = layer_of(k)
        data = point_data[:, pl.ds(pl.multiple_of(m * WIDE, 128), WIDE)]
        key = data[5:6].astype(jnp.int32).astype(jnp.int16)
        chosen = jnp.where(key_row == key, BF16(1), BF16(0)).astype(FP8)
        picked = dot(y_part[...], chosen, ((1,), (0,)))
        picked = picked[0:2 * BOTH] + (picked[2 * BOTH:4 * BOTH] + picked[4 * BOTH:])
        re0, re1, im0, im1 = (picked[i * PAIRS:(i + 1) * PAIRS] for i in range(4))
        turned = data * unfit
        cos0, sin0, cos1, sin1 = (turned[i:i + 1] for i in range(4))
        signed = turned * data[4:5]
        cos0_im, sin0_im, cos1_im, sin1_im = (signed[i:i + 1] for i in range(4))
        real = cos0 * re0 + sin0 * im0 + cos1 * re1 + sin1 * im1
        imag = cos0_im * im0 - sin0_im * re0 + cos1_im * im1 - sin1_im * re1
        for n in range(2):
            at = n * CHIP_POINTS
            middle_re, middle_im = real[:, at + 128:at + 256], imag[:, at + 128:at + 256]
            for side in range(2):
                if side == 0:
                    middle = jnp.where(half_lane, middle_re, pltpu.roll(middle_im, NG, 1))
                else:
                    middle = jnp.where(half_lane, pltpu.roll(middle_re, NG, 1), middle_im)
                lanes = slice(at + 256 * side, at + 256 * side + 128)
                own[side, 2 * m + n] = jnp.concatenate(
                    [real[:, lanes], imag[:, lanes], middle, bound_rows], 0
                )

    def hand_over(k):
        for n in range(2):
            to_sibling(2 * layer_of(k) + n).start()

    def send(k):
        for n in range(2):
            to_chip(2 * layer_of(k) + n).start()

    def scaled(slab):
        slab = slab.astype(jnp.int32).astype(F32)
        return slab * jnp.exp2(slab[120:121] - 15.0)

    def add_chips(k, total):
        for n in range(2):
            j = 2 * ((2 * z - layer_of(k) + 8) % 8) + n
            remote(
                chip_out.at[j], chip_in.at[j], chip_send.at[j], chip_recv.at[j], (2 * j + core, g)
            ).wait_recv()
            total = total + scaled(chip_in[j])
        return total

    def select_first(k, _):
        select(k)
        hand_over(k)
        return 0

    def select_and_add(k, _):
        select(k)
        hand_over(k)
        arrive(k - 1)
        add_core(k - 1)
        send(k - 1)
        return 0

    def select_and_sum(k, total):
        select_and_add(k, 0)
        return add_chips(k - 8, total)

    lax.fori_loop(0, 1, select_first, 0)
    lax.fori_loop(1, 8, select_and_add, 0)
    total = lax.fori_loop(8, 8, select_and_sum, jnp.zeros((128, 128), F32))
    arrive(7)
    add_core(7)
    to_chip(2 * z + 1 - x).start()
    total = lax.fori_loop(0, 7, add_chips, total + scaled(chip_out[chip]))
    remote(
        chip_out.at[partner], chip_in.at[partner], chip_send.at[partner], chip_recv.at[partner],
        (2 * partner + core, g),
    ).wait_recv()
    total = total + scaled(chip_in[partner])
    block[...] = jnp.where(tail, 0.0, total).astype(BF16)

    def to_z(k):
        other = (z + k) % 8
        return remote(
            block, z_blocks.at[z], z_send.at[other], z_recv.at[z], (other * 4 + x * 2 + core, g)
        )

    def to_row(k):
        other = (g + k) % 8
        return remote(block, row_blocks.at[g], row_send.at[other], row_recv.at[g], (f, other))

    def send_block(k, _):
        to_z(k).start()
        to_row(k).start()
        return 0

    lax.fori_loop(1, 8, send_block, 0)
    z_blocks[z] = block[...]
    row_blocks[g] = block[...]

    def to_plane(layer, to_x):
        return remote(
            z_blocks.at[layer], col_blocks.at[core, x, g],
            plane_send.at[layer, to_x], plane_recv.at[x, g], (z * 4 + to_x * 2 + core, layer),
        )

    def stays(layer, to_x):
        return jnp.logical_and(layer == g, to_x == x)

    def spread(k, _):
        layer = (z + (k + 1) // 2 * (1 - 2 * (k % 2)) + 8) % 8

        @pl.when(k > 0)
        def _():
            remote(
                block, z_blocks.at[layer], z_send.at[layer], z_recv.at[layer],
                (layer * 4 + x * 2 + core, g),
            ).wait_recv()

        for to_x in range(2):
            @pl.when(stays(layer, to_x))
            def _():
                col_blocks[core, x, g] = z_blocks[layer]

            @pl.when(jnp.logical_not(stays(layer, to_x)))
            def _():
                to_plane(layer, to_x).start()

        return 0

    lax.fori_loop(0, 8, spread, 0)

    def relay(side, from_x, from_g):
        return remote(
            col_blocks.at[side, from_x, from_g], col_blocks.at[side, from_x, from_g],
            relay_send.at[from_x, from_g], relay_recv.at[from_x, from_g], (sibling, g),
        )

    def pass_on(k, _):
        from_x, from_g = (x + k) % 2, (g + k // 2) % 8

        @pl.when(k > 0)
        def _():
            remote(
                z_blocks.at[0], col_blocks.at[core, from_x, from_g],
                plane_send.at[0, 0], plane_recv.at[from_x, from_g],
                (z * 4 + from_x * 2 + core, from_g),
            ).wait_recv()

        relay(core, from_x, from_g).start()
        return 0

    lax.fori_loop(0, 16, pass_on, 0)

    def row_arrives(k, _):
        other = (g + k) % 8
        remote(
            block, row_blocks.at[other], row_send.at[other], row_recv.at[other], (f, other)
        ).wait_recv()
        return 0

    lax.fori_loop(1, 8, row_arrives, 0)

    stores[0].start()
    stores[1].start()

    def relay_arrives(k, _):
        relay(1 - core, k % 2, k // 2).wait_recv()
        return 0

    lax.fori_loop(0, 16, relay_arrives, 0)
    stores[2].start()

    stores[0].wait()
    stores[1].wait()
    stores[2].wait()

    def drain_chips(k, _):
        to_sibling((chip + k) % CHIPS).wait_send()

        @pl.when(k < CHIPS)
        def _():
            to_chip((chip + k) % CHIPS).wait_send()

        return 0

    lax.fori_loop(1, CHIPS + 1, drain_chips, 0)

    def drain_blocks(k, _):
        to_z(k).wait_send()
        to_row(k).wait_send()
        return 0

    lax.fori_loop(1, 8, drain_blocks, 0)

    def drain_plane(k, _):
        @pl.when(jnp.logical_not(stays(k // 2, k % 2)))
        def _():
            to_plane(k // 2, k % 2).wait_send()

        relay(core, k % 2, k // 2).wait_send()
        return 0

    lax.fori_loop(0, 16, drain_plane, 0)


def product_kernel(rows_in, columns_in, chi_real, chi_imag):
    core = lax.axis_index("fft") % 2
    half_lane = lax.broadcasted_iota(jnp.int32, (8 * PAIRS, 128), 1) < NG

    def gather(read):
        blocks = [read(i).astype(F32) for i in range(8)]
        return tuple(
            jnp.concatenate([b[s * PAIRS:(s + 1) * PAIRS] for b in blocks], 0) for s in range(3)
        )

    real, imag, middle = gather(lambda i: rows_in[i])
    full = jnp.concatenate([real, imag], 0).astype(BF16)
    half = jnp.concatenate([middle, pltpu.roll(middle, NG, 1)], 0)[:, 0:NG].astype(BF16)
    full_row = pl.multiple_of(core * NG, NG)
    half_row = pl.multiple_of((1 - core) * 128, NG)
    real0, imag0, middle0 = gather(lambda i: columns_in[0, 0, i])
    real2, imag2, middle2 = gather(lambda i: columns_in[1, 0, i])
    real1 = jnp.where(half_lane, middle0, pltpu.roll(middle2, NG, 1))
    imag1 = jnp.where(half_lane, pltpu.roll(middle0, NG, 1), middle2)
    real = jnp.concatenate([real0, real1, real2], 1)
    imag = jnp.concatenate([imag0, imag1, imag2], 1)
    right_sum = jnp.concatenate([real, imag], 0).astype(BF16)
    right_cross = jnp.concatenate([imag, -real], 0).astype(BF16)
    for left, rows in ((full, pl.ds(full_row, 128)), (half, pl.ds(half_row, NG))):
        chi_real[rows, :] = -dot(left, right_sum, ((0,), (0,)))
        chi_imag[rows, :] = dot(left, right_cross, ((0,), (0,)))


def product(rows, columns, shape):
    count, width = shape.shape
    out = pl.BlockSpec((count, CHIP_POINTS), lambda side: (0, side))
    return pl.pallas_call(
        product_kernel,
        grid=(width // CHIP_POINTS,),
        out_shape=(shape, shape),
        in_specs=[
            pl.BlockSpec((8, 128, 128), lambda side: (0, 0, 0)),
            pl.BlockSpec((2, 1, 8, 128, 128), lambda side: (0, side, 0, 0, 0)),
        ],
        out_specs=(out, out),
        compiler_params=pltpu.CompilerParams(vmem_limit_bytes=56 * 1024 * 1024),
    )(rows, columns)


def per_device(
    psi_valence,
    psi_conduction,
    energy_valence,
    energy_conduction,
    pair_valence,
    pair_conduction,
    g_index,
):
    def tiles(psi):
        bands = psi.shape[0]
        return psi.reshape(bands, 2, 32, 128).transpose(0, 2, 1, 3).reshape(bands, NG, 128)

    psi_c, psi_v = tiles(psi_conduction), tiles(psi_valence)
    points = g_index.shape[0]
    shape = jax.ShapeDtypeStruct(
        (points // lax.axis_size("fft"), points // lax.axis_size("grp")), F32
    )
    smem = pl.BlockSpec(memory_space=pltpu.SMEM)
    vmem = pl.BlockSpec(memory_space=pltpu.VMEM)
    anywhere = pl.BlockSpec(memory_space=pl.ANY)
    dma = pltpu.SemaphoreType.DMA

    slabs = pltpu.VMEM((CHIPS, 128, 128), jnp.int16)
    blocks = pltpu.VMEM((8, 128, 128), BF16)
    rows, columns = pl.pallas_call(
        functools.partial(kernel, PAIRS * lax.axis_size("grp")),
        out_shape=(
            jax.ShapeDtypeStruct((8, 128, 128), BF16),
            jax.ShapeDtypeStruct((2, 2, 8, 128, 128), BF16),
        ),
        in_specs=[smem] * 4 + [anywhere] * 2 + [vmem] * 4,
        out_specs=(anywhere, anywhere),
        scratch_shapes=[
            pltpu.VMEM(psi_v.shape, BF16),
            *[pltpu.VMEM((psi_c.shape[0], PIECE, 128), BF16)] * LOADS,
            pltpu.VMEM((PAIRS * NG, 128), F32),
            pltpu.VMEM((HALF_C, 128, 128), F32),
            pltpu.VMEM((6 * BOTH, KEYS), FP8),
            pltpu.VMEM((8, points), F32),
            pltpu.VMEM((2, CHIPS, 128, 128), F32),
            pltpu.VMEM((CHIPS, 128, 128), F32),
            slabs, slabs,
            pltpu.VMEM((128, 128), BF16),
            blocks, blocks,
            pltpu.VMEM((2, 2, 8, 128, 128), BF16),
            dma((8 + LOADS,)),
            dma((CHIPS,)), dma((CHIPS,)), dma((CHIPS,)), dma((CHIPS,)),
            dma((8,)), dma((8,)), dma((8,)), dma((8,)),
            dma((8, 2)), dma((2, 8)), dma((2, 8)), dma((2, 8)),
        ],
        compiler_params=pltpu.CompilerParams(
            collective_id=0, has_side_effects=True, vmem_limit_bytes=62 * 1024 * 1024
        ),
    )(
        pair_conduction, pair_valence, energy_conduction, energy_valence, psi_c, psi_v,
        jnp.asarray(table_z()), jnp.asarray(table_y()), jnp.asarray(table_x()),
        g_index.reshape(1, -1),
    )
    return product(rows, columns, shape)


def solution(mesh):
    placed = (P(None, "fft", None), P(None, "fft", None), P(), P(), P("grp"), P("grp"), P())
    return jax.shard_map(
        per_device,
        mesh=mesh,
        in_specs=placed,
        out_specs=(P("fft", "grp"), P("fft", "grp")),
        check_vma=False,
    )
```

time: 55.7 us -> 54.1 us (0.971)
  local copies, waits for them, and re-layouts: 3.83 us -> 0 us
  Pallas kernels: 50.6 us -> 52.8 us
    unnamed x2 -> x0, local copies, waits for them, and re-layouts: 3.83 us -> none
    pallas_call x0 -> x1, Pallas kernels: none -> 3.09 us  [product(): pl.pallas_call(product_kernel, grid=(width // CHIP_POINTS,), out_shape=(s...]
    pallas_call x1, Pallas kernels: 50.6 us -> 49.7 us  [per_device(): pl.pallas_call(functools.partial(kernel, PAIRS * lax.axis_size('grp')), o...]
where the time goes in v4:
time: 54.1 us; the launch traced here: 53.5 us
  Pallas kernels  52.8 us (98%)
  between operations  0.64 us (1%)
    pallas_call x1, Pallas kernels, per_device(): pl.pallas_call(functools.partial(kernel, PAIRS * lax.axis_size('grp')), o...  49.7 us
    pallas_call x1, Pallas kernels, product(): pl.pallas_call(product_kernel, grid=(width // CHIP_POINTS,), out_shape=(s...  3.09 us

profile of v4, /device:TPU:13, one launch (start us, length us, event | category | flops | bytes accessed | tf_op | source)
XLA Modules:
  0.0 53.5 jit_solution(18371834752572038478)
XLA Ops:
  0.6 49.7 %shard_map.113 = (bf16[8,128,128]{2,1,0:T(8,128)(2,1)}, bf16[2,2,8,128,128]{4,3,2,1,0:T(8,128)(2,1)}) custom-call(s32[40]{0:T(128)} %pair_c.1, s32[40]{0:T(128)} %pair_v.1, f32[384]{0:T(512)} %energy_c.1, f32[16]{0:T(128)} %energy_v.1, bf16[384,64,128]{2,1,0:T(8,128)(2,1)} %bitcast.11, bf16[16,64,128]{2,1,0:T(8,128)(2,1)} %bitcast.12, ...), custom_call_target="tpu_custom_call" | custom-call | tf_op jit(solution)/shard_map/pallas_call | solution.py:527
  50.4 3.1 %shard_map.114 = (f32[192,768]{1,0:T(8,128)}, f32[192,768]{1,0:T(8,128)}) custom-call(bf16[8,128,128]{2,1,0:T(8,128)(2,1)} %get-tuple-element.4.rows_in, bf16[2,2,8,128,128]{4,3,2,1,0:T(8,128)(2,1)} %get-tuple-element.5.columns_in), custom_call_target="tpu_custom_call" | custom-call | tf_op jit(solution)/shard_map/pallas_call | solution.py:489

commit v5 on v4

--- a/solution.py
+++ b/solution.py
@@ -16,6 +16,7 @@
 PAIRS = 40
 BOTH = 2 * PAIRS
 CHIPS = 16
+JOIN_LAG = 3
 LOADS = 4
 PIECE = NG // LOADS
 CHIP_POINTS = 384
@@ -80,8 +81,8 @@
     psi_c, psi_v, wz, wy, wx, g_index,
     rows_out, columns_out,
     band_v, band_c0, band_c1, band_c2, band_c3, density, z_part, y_part, point_data,
-    own, core_in, chip_out, chip_in, block, z_blocks, row_blocks, col_blocks, load,
-    core_send, core_recv, chip_send, chip_recv, z_send, z_recv,
+    own, core_in, sums, x_out, x_in, chip_out, chip_in, block, z_blocks, row_blocks, col_blocks, load,
+    x_send, x_recv, core_send, core_recv, chip_send, chip_recv, z_send, z_recv,
     row_send, row_recv, plane_send, plane_recv, relay_send, relay_recv,
 ):
     f, g = lax.axis_index("fft"), lax.axis_index("grp")
@@ -243,13 +244,39 @@
         for n in range(2):
             to_sibling(2 * layer_of(k) + n).wait_recv()
 
+    def rounded(total, bound):
+        level = jnp.floor(jnp.log2(bound * 1.001)) + 1.0
+        total = jnp.where(tail, level, jnp.floor(total * jnp.exp2(15.0 - level) + 0.5))
+        return total.astype(jnp.int32).astype(jnp.int16)
+
     def add_core(k):
         for n in range(2):
             j = 2 * layer_of(k) + n
             total = own[core, j] + core_in[j]
-            level = jnp.floor(jnp.log2(total[120:121] * 1.001)) + 1.0
-            total = jnp.where(tail, level, jnp.floor(total * jnp.exp2(15.0 - level) + 0.5))
-            chip_out[j] = total.astype(jnp.int32).astype(jnp.int16)
+            chip_out[j] = rounded(total, total[120:121])
+
+    def to_partner(m):
+        return remote(
+            x_out.at[m], x_in.at[m], x_send.at[m], x_recv.at[m], (2 * partner + core, g)
+        )
+
+    def add_far(k):
+        m = layer_of(k)
+        mine, other = 2 * m + x, 2 * m + 1 - x
+        total = own[core, other] + core_in[other]
+        x_out[m] = rounded(total, total[120:121])
+        to_partner(m).start()
+        sums[m] = own[core, mine] + core_in[mine]
+
+    def join(k):
+        m = layer_of(k)
+        to_partner(m).wait_recv()
+        theirs = x_in[m].astype(jnp.int32).astype(F32)
+        theirs_level = theirs[120:121]
+        total = sums[m] + theirs * jnp.exp2(theirs_level - 15.0)
+        bound = sums[m, 120:121] + jnp.exp2(theirs_level)
+        chip_out[2 * m + x] = rounded(total, bound)
+        to_chip(2 * m + x).start()
 
     def select(k):
         m = layer_of(k)
@@ -290,44 +317,52 @@
         slab = slab.astype(jnp.int32).astype(F32)
         return slab * jnp.exp2(slab[120:121] - 15.0)
 
+    def chip_arrives(j, total):
+        remote(
+            chip_out.at[j], chip_in.at[j], chip_send.at[j], chip_recv.at[j], (2 * j + core, g)
+        ).wait_recv()
+        return total + scaled(chip_in[j])
+
     def add_chips(k, total):
-        for n in range(2):
-            j = 2 * ((2 * z - layer_of(k) + 8) % 8) + n
-            remote(
-                chip_out.at[j], chip_in.at[j], chip_send.at[j], chip_recv.at[j], (2 * j + core, g)
-            ).wait_recv()
-            total = total + scaled(chip_in[j])
-        return total
-
-    def select_first(k, _):
-        select(k)
-        hand_over(k)
-        return 0
-
-    def select_and_add(k, _):
+        layer = (2 * z - layer_of(k) + 8) % 8
+        return chip_arrives(2 * layer + 1, chip_arrives(2 * layer, total))
+
+    def add_joined(k, total):
+        return chip_arrives(2 * ((2 * z - layer_of(k) + 8) % 8) + x, total)
+
+    def loop(first, last, body):
+        def run(k, _):
+            body(k)
+            return 0
+
+        lax.fori_loop(first, last, run, 0)
+
+    def step(k, far, joins):
         select(k)
         hand_over(k)
         arrive(k - 1)
-        add_core(k - 1)
-        send(k - 1)
-        return 0
-
-    def select_and_sum(k, total):
-        select_and_add(k, 0)
-        return add_chips(k - 8, total)
-
-    lax.fori_loop(0, 1, select_first, 0)
-    lax.fori_loop(1, 8, select_and_add, 0)
-    total = lax.fori_loop(8, 8, select_and_sum, jnp.zeros((128, 128), F32))
+        if far:
+            add_far(k - 1)
+        else:
+            add_core(k - 1)
+            send(k - 1)
+        if joins:
+            join(k - JOIN_LAG)
+
+    select(0)
+    hand_over(0)
+    step(1, False, False)
+    loop(2, 1 + JOIN_LAG, lambda k: step(k, True, False))
+    loop(1 + JOIN_LAG, 6, lambda k: step(k, True, True))
+    loop(6, 8, lambda k: step(k, False, True))
     arrive(7)
     add_core(7)
     to_chip(2 * z + 1 - x).start()
-    total = lax.fori_loop(0, 7, add_chips, total + scaled(chip_out[chip]))
-    remote(
-        chip_out.at[partner], chip_in.at[partner], chip_send.at[partner], chip_recv.at[partner],
-        (2 * partner + core, g),
-    ).wait_recv()
-    total = total + scaled(chip_in[partner])
+    loop(8 - JOIN_LAG, 5, join)
+    total = add_chips(0, scaled(chip_out[chip]))
+    total = lax.fori_loop(1, 5, add_joined, total)
+    total = lax.fori_loop(5, 7, add_chips, total)
+    total = chip_arrives(partner, total)
     block[...] = jnp.where(tail, 0.0, total).astype(BF16)
 
     def to_z(k):
@@ -340,12 +375,19 @@
         other = (g + k) % 8
         return remote(block, row_blocks.at[g], row_send.at[other], row_recv.at[g], (f, other))
 
-    def send_block(k, _):
-        to_z(k).start()
+    def near(k):
+        return (k + 1) // 2 * (1 - 2 * (k % 2)) + 8
+
+    def send_z(k, _):
+        to_z(near(k)).start()
+        return 0
+
+    def send_row(k, _):
         to_row(k).start()
         return 0
 
-    lax.fori_loop(1, 8, send_block, 0)
+    lax.fori_loop(1, 8, send_z, 0)
+    lax.fori_loop(1, 8, send_row, 0)
     z_blocks[z] = block[...]
     row_blocks[g] = block[...]
 
@@ -359,7 +401,7 @@
         return jnp.logical_and(layer == g, to_x == x)
 
     def spread(k, _):
-        layer = (z + (k + 1) // 2 * (1 - 2 * (k % 2)) + 8) % 8
+        layer = (z + near(k)) % 8
 
         @pl.when(k > 0)
         def _():
@@ -426,16 +468,14 @@
     stores[1].wait()
     stores[2].wait()
 
-    def drain_chips(k, _):
-        to_sibling((chip + k) % CHIPS).wait_send()
-
-        @pl.when(k < CHIPS)
-        def _():
-            to_chip((chip + k) % CHIPS).wait_send()
-
-        return 0
-
-    lax.fori_loop(1, CHIPS + 1, drain_chips, 0)
+    loop(0, CHIPS, lambda j: to_sibling(j).wait_send())
+    for k in (0, 5, 6):
+        for n in range(2):
+            to_chip(2 * layer_of(k) + n).wait_send()
+    for k in range(1, 5):
+        to_partner(layer_of(k)).wait_send()
+        to_chip(2 * layer_of(k) + x).wait_send()
+    to_chip(2 * z + 1 - x).wait_send()
 
     def drain_blocks(k, _):
         to_z(k).wait_send()
@@ -541,11 +581,14 @@
             pltpu.VMEM((8, points), F32),
             pltpu.VMEM((2, CHIPS, 128, 128), F32),
             pltpu.VMEM((CHIPS, 128, 128), F32),
+            pltpu.VMEM((8, 128, 128), F32),
+            pltpu.VMEM((8, 128, 128), jnp.int16), pltpu.VMEM((8, 128, 128), jnp.int16),
             slabs, slabs,
             pltpu.VMEM((128, 128), BF16),
             blocks, blocks,
             pltpu.VMEM((2, 2, 8, 128, 128), BF16),
             dma((8 + LOADS,)),
+            dma((8,)), dma((8,)),
             dma((CHIPS,)), dma((CHIPS,)), dma((CHIPS,)), dma((CHIPS,)),
             dma((8,)), dma((8,)), dma((8,)), dma((8,)),
             dma((8, 2)), dma((2, 8)), dma((2, 8)), dma((2, 8)),

time: 54.1 us -> 51.9 us (0.959)
  Pallas kernels: 52.8 us -> 51.1 us
    pallas_call x1, Pallas kernels: 49.7 us -> 48 us  [per_device(): pl.pallas_call(functools.partial(kernel, PAIRS * lax.axis_size('grp')), o...]
where the time goes in v5:
time: 51.9 us; the launch traced here: 51.7 us
  Pallas kernels  51.1 us (98%)
  between operations  0.64 us (1%)
    pallas_call x1, Pallas kernels, per_device(): pl.pallas_call(functools.partial(kernel, PAIRS * lax.axis_size('grp')), o...  48 us
    pallas_call x1, Pallas kernels, product(): pl.pallas_call(product_kernel, grid=(width // CHIP_POINTS,), out_shape=(s...  3.09 us

profile of v5, /device:TPU:13, one launch (start us, length us, event | category | flops | bytes accessed | tf_op | source)
XLA Modules:
  0.0 51.7 jit_solution(17153108821792237272)
XLA Ops:
  0.6 48.0 %shard_map.113 = (bf16[8,128,128]{2,1,0:T(8,128)(2,1)}, bf16[2,2,8,128,128]{4,3,2,1,0:T(8,128)(2,1)}) custom-call(s32[40]{0:T(128)} %pair_c.1, s32[40]{0:T(128)} %pair_v.1, f32[384]{0:T(512)} %energy_c.1, f32[16]{0:T(128)} %energy_v.1, bf16[384,64,128]{2,1,0:T(8,128)(2,1)} %bitcast.11, bf16[16,64,128]{2,1,0:T(8,128)(2,1)} %bitcast.12, ...), custom_call_target="tpu_custom_call" | custom-call | tf_op jit(solution)/shard_map/pallas_call | solution.py:567
  48.6 3.1 %shard_map.114 = (f32[192,768]{1,0:T(8,128)}, f32[192,768]{1,0:T(8,128)}) custom-call(bf16[8,128,128]{2,1,0:T(8,128)(2,1)} %get-tuple-element.4.rows_in, bf16[2,2,8,128,128]{4,3,2,1,0:T(8,128)(2,1)} %get-tuple-element.5.columns_in), custom_call_target="tpu_custom_call" | custom-call | tf_op jit(solution)/shard_map/pallas_call | solution.py:529

commit v6 on v5

--- a/solution.py
+++ b/solution.py
@@ -421,53 +421,7 @@
 
         return 0
 
-    lax.fori_loop(0, 8, spread, 0)
-
-    def relay(side, from_x, from_g):
-        return remote(
-            col_blocks.at[side, from_x, from_g], col_blocks.at[side, from_x, from_g],
-            relay_send.at[from_x, from_g], relay_recv.at[from_x, from_g], (sibling, g),
-        )
-
-    def pass_on(k, _):
-        from_x, from_g = (x + k) % 2, (g + k // 2) % 8
-
-        @pl.when(k > 0)
-        def _():
-            remote(
-                z_blocks.at[0], col_blocks.at[core, from_x, from_g],
-                plane_send.at[0, 0], plane_recv.at[from_x, from_g],
-                (z * 4 + from_x * 2 + core, from_g),
-            ).wait_recv()
-
-        relay(core, from_x, from_g).start()
-        return 0
-
-    lax.fori_loop(0, 16, pass_on, 0)
-
-    def row_arrives(k, _):
-        other = (g + k) % 8
-        remote(
-            block, row_blocks.at[other], row_send.at[other], row_recv.at[other], (f, other)
-        ).wait_recv()
-        return 0
-
-    lax.fori_loop(1, 8, row_arrives, 0)
-
-    stores[0].start()
-    stores[1].start()
-
-    def relay_arrives(k, _):
-        relay(1 - core, k % 2, k // 2).wait_recv()
-        return 0
-
-    lax.fori_loop(0, 16, relay_arrives, 0)
-    stores[2].start()
-
-    stores[0].wait()
-    stores[1].wait()
-    stores[2].wait()
-
+    spread(0, 0)
     loop(0, CHIPS, lambda j: to_sibling(j).wait_send())
     for k in (0, 5, 6):
         for n in range(2):
@@ -476,6 +430,7 @@
         to_partner(layer_of(k)).wait_send()
         to_chip(2 * layer_of(k) + x).wait_send()
     to_chip(2 * z + 1 - x).wait_send()
+    lax.fori_loop(1, 8, spread, 0)
 
     def drain_blocks(k, _):
         to_z(k).wait_send()
@@ -483,17 +438,61 @@
         return 0
 
     lax.fori_loop(1, 8, drain_blocks, 0)
+
+    def row_arrives(k, _):
+        other = (g + k) % 8
+        remote(
+            block, row_blocks.at[other], row_send.at[other], row_recv.at[other], (f, other)
+        ).wait_recv()
+        return 0
+
+    lax.fori_loop(1, 8, row_arrives, 0)
+    stores[0].start()
+
+    def relay(side, from_x, from_g):
+        return remote(
+            col_blocks.at[side, from_x, from_g], col_blocks.at[side, from_x, from_g],
+            relay_send.at[from_x, from_g], relay_recv.at[from_x, from_g], (sibling, g),
+        )
+
+    def pass_on(k, _):
+        from_x, from_g = (x + k) % 2, (g + k // 2) % 8
+
+        @pl.when(k > 0)
+        def _():
+            remote(
+                z_blocks.at[0], col_blocks.at[core, from_x, from_g],
+                plane_send.at[0, 0], plane_recv.at[from_x, from_g],
+                (z * 4 + from_x * 2 + core, from_g),
+            ).wait_recv()
+
+        relay(core, from_x, from_g).start()
+        return 0
+
+    lax.fori_loop(0, 16, pass_on, 0)
 
     def drain_plane(k, _):
         @pl.when(jnp.logical_not(stays(k // 2, k % 2)))
         def _():
             to_plane(k // 2, k % 2).wait_send()
 
-        relay(core, k % 2, k // 2).wait_send()
         return 0
 
     lax.fori_loop(0, 16, drain_plane, 0)
 
+    stores[1].start()
+
+    def relay_arrives(k, _):
+        relay(1 - core, k % 2, k // 2).wait_recv()
+        return 0
+
+    lax.fori_loop(0, 16, relay_arrives, 0)
+    stores[2].start()
+
+    loop(0, 16, lambda k: relay(core, k % 2, k // 2).wait_send())
+    stores[0].wait()
+    stores[1].wait()
+    stores[2].wait()
 
 def product_kernel(rows_in, columns_in, chi_real, chi_imag):
     core = lax.axis_index("fft") % 2

time: 51.9 us -> 51.3 us (0.988)
    pallas_call x1, Pallas kernels: 48 us -> 47.5 us  [per_device(): pl.pallas_call(functools.partial(kernel, PAIRS * lax.axis_size('grp')), o...]
where the time goes in v6:
time: 51.3 us; the launch traced here: 51.2 us
  Pallas kernels  50.6 us (99%)
  between operations  0.64 us (1%)
    pallas_call x1, Pallas kernels, per_device(): pl.pallas_call(functools.partial(kernel, PAIRS * lax.axis_size('grp')), o...  47.5 us
    pallas_call x1, Pallas kernels, product(): pl.pallas_call(product_kernel, grid=(width // CHIP_POINTS,), out_shape=(s...  3.08 us

profile of v6, /device:TPU:13, one launch (start us, length us, event | category | flops | bytes accessed | tf_op | source)
XLA Modules:
  0.0 51.2 jit_solution(1325714822560532902)
XLA Ops:
  0.6 47.5 %shard_map.113 = (bf16[8,128,128]{2,1,0:T(8,128)(2,1)}, bf16[2,2,8,128,128]{4,3,2,1,0:T(8,128)(2,1)}) custom-call(s32[40]{0:T(128)} %pair_c.1, s32[40]{0:T(128)} %pair_v.1, f32[384]{0:T(512)} %energy_c.1, f32[16]{0:T(128)} %energy_v.1, bf16[384,64,128]{2,1,0:T(8,128)(2,1)} %bitcast.11, bf16[16,64,128]{2,1,0:T(8,128)(2,1)} %bitcast.12, ...), custom_call_target="tpu_custom_call" | custom-call | tf_op jit(solution)/shard_map/pallas_call | solution.py:566
  48.1 3.1 %shard_map.114 = (f32[192,768]{1,0:T(8,128)}, f32[192,768]{1,0:T(8,128)}) custom-call(bf16[8,128,128]{2,1,0:T(8,128)(2,1)} %get-tuple-element.4.rows_in, bf16[2,2,8,128,128]{4,3,2,1,0:T(8,128)(2,1)} %get-tuple-element.5.columns_in), custom_call_target="tpu_custom_call" | custom-call | tf_op jit(solution)/shard_map/pallas_call | solution.py:528

commit v7 on v6

--- a/solution.py
+++ b/solution.py
@@ -105,7 +105,12 @@
     stores = [
         pltpu.make_async_copy(row_blocks, rows_out, load.at[2]),
         pltpu.make_async_copy(col_blocks.at[core], columns_out.at[core], load.at[3]),
-        pltpu.make_async_copy(col_blocks.at[1 - core], columns_out.at[1 - core], load.at[4]),
+        *(
+            pltpu.make_async_copy(
+                col_blocks.at[1 - core, n], columns_out.at[1 - core, n], load.at[4 + n]
+            )
+            for n in range(2)
+        ),
     ]
 
     def remote(src, dst, send, recv, to):
@@ -483,16 +488,19 @@
     stores[1].start()
 
     def relay_arrives(k, _):
-        relay(1 - core, k % 2, k // 2).wait_recv()
-        return 0
-
-    lax.fori_loop(0, 16, relay_arrives, 0)
+        relay(1 - core, k // 8, k % 8).wait_recv()
+        return 0
+
+    lax.fori_loop(0, 8, relay_arrives, 0)
     stores[2].start()
+    lax.fori_loop(8, 16, relay_arrives, 0)
+    stores[3].start()
 
     loop(0, 16, lambda k: relay(core, k % 2, k // 2).wait_send())
     stores[0].wait()
     stores[1].wait()
     stores[2].wait()
+    stores[3].wait()
 
 def product_kernel(rows_in, columns_in, chi_real, chi_imag):
     core = lax.axis_index("fft") % 2

time: 51.3 us -> 51.3 us (level)
  no operation moved by 1% of the time
where the time goes in v7:
time: 51.3 us; the launch traced here: 51.1 us
  Pallas kernels  50.5 us (98%)
  between operations  0.64 us (1%)
    pallas_call x1, Pallas kernels, per_device(): pl.pallas_call(functools.partial(kernel, PAIRS * lax.axis_size('grp')), o...  47.4 us
    pallas_call x1, Pallas kernels, product(): pl.pallas_call(product_kernel, grid=(width // CHIP_POINTS,), out_shape=(s...  3.1 us

profile of v7, /device:TPU:13, one launch (start us, length us, event | category | flops | bytes accessed | tf_op | source)
XLA Modules:
  0.0 51.1 jit_solution(1898100316333734883)
XLA Ops:
  0.6 47.4 %shard_map.113 = (bf16[8,128,128]{2,1,0:T(8,128)(2,1)}, bf16[2,2,8,128,128]{4,3,2,1,0:T(8,128)(2,1)}) custom-call(s32[40]{0:T(128)} %pair_c.1, s32[40]{0:T(128)} %pair_v.1, f32[384]{0:T(512)} %energy_c.1, f32[16]{0:T(128)} %energy_v.1, bf16[384,64,128]{2,1,0:T(8,128)(2,1)} %bitcast.11, bf16[16,64,128]{2,1,0:T(8,128)(2,1)} %bitcast.12, ...), custom_call_target="tpu_custom_call" | custom-call | tf_op jit(solution)/shard_map/pallas_call | solution.py:574
  48.1 3.1 %shard_map.114 = (f32[192,768]{1,0:T(8,128)}, f32[192,768]{1,0:T(8,128)}) custom-call(bf16[8,128,128]{2,1,0:T(8,128)(2,1)} %get-tuple-element.4.rows_in, bf16[2,2,8,128,128]{4,3,2,1,0:T(8,128)(2,1)} %get-tuple-element.5.columns_in), custom_call_target="tpu_custom_call" | custom-call | tf_op jit(solution)/shard_map/pallas_call | solution.py:536
